TPU v7x, 32 devices: a whole 2x2x4 slice. The times are simulated.
32 devices in a mesh: ctx: 8 (over z, x), tp: 4 (over y, core).
Axes of the slice: x: 2, y: 2, z: 4, core: 2. Of those that a mesh axis runs over, the one named last changes fastest.
Arguments:
- queries: bfloat16 [2048, 2048], P('ctx', 'tp'), may hold values from -6 to 6
- keys: bfloat16 [2048, 2048], P('ctx', 'tp'), may hold values from -6 to 6
- values: bfloat16 [2048, 2048], P('ctx', 'tp'), may hold values from -6 to 6
- out_grad: bfloat16 [2048, 4096], P('ctx', 'tp'), may hold values from -6 to 6
- w_out: bfloat16 [2048, 4096], P('tp'), may hold values from -0.09375 to 0.09375
- offsets: int32 [16, 3], P('tp'), may hold values from 0 to 3, as said below
Outputs:
- query_grad: bfloat16 [2048, 2048], P('ctx', 'tp')
- key_grad: bfloat16 [2048, 2048], P('ctx', 'tp')
- value_grad: bfloat16 [2048, 2048], P('ctx', 'tp')
Inputs may be any that keep to these rules, and one draw needn't show every extreme that they name: offsets[h, l] lies between 0 and 2^l - 1.
All inputs are finite; a program needn't handle non-finite values.
Results may differ from a plain program's by a relative error of at most 0.017.
Values may be sent and summed in bfloat16 or wider, within the bound.
A program may use at most 64 MiB of HBM per device.

v0:
```python
from functools import reduce
import math

import jax
import jax.numpy as jnp
from jax import lax
from jax.sharding import PartitionSpec as P

LEVELS = 3
KEYS_SEG = 1024


NEGATIVE_FILL = -1e30


def for_sending(array):

    def short(part):
        return part.astype(jnp.bfloat16) if part.dtype == jnp.float32 else part

    return jax.tree.map(short, array)


def passed_along(block, axis, distance):
    devices = range(lax.axis_size(axis))
    route = [((i - distance) % len(devices), i) for i in devices]
    return lax.ppermute(block, axis, route)


def pick_table(offset_col, stride):
    return lax.broadcasted_iota(jnp.int32, (stride, offset_col.shape[0]), 0) == offset_col[None, :]


def pack_rows(whole, pick):
    stride = pick.shape[0]
    grouped = whole.reshape((whole.shape[0] // stride, stride) + whole.shape[1:])
    chosen = pick.reshape((1,) + pick.shape + (1,) * (whole.ndim - 2))
    return jnp.sum(jnp.where(chosen, grouped, jnp.zeros((), whole.dtype)), axis=1)


def spread_rows(packed, pick, fill_value):
    stride = pick.shape[0]
    chosen = pick.reshape((1,) + pick.shape + (1,) * (packed.ndim - 2))
    spread = jnp.where(chosen, packed[:, None], jnp.asarray(fill_value, packed.dtype))
    return spread.reshape((packed.shape[0] * stride,) + packed.shape[1:])


def linked_pairs(offset_col, stride, segment, query_start, key_start, row_count):
    tok_rows = row_count * stride
    total_rows = tok_rows * lax.axis_size("ctx")
    rotation = 2 * tok_rows
    lanes = lax.broadcasted_iota(jnp.int32, (row_count,), 0) * stride
    query_pos = (
        query_start + lanes[None, :, None] + offset_col[:, None, None] - rotation
    ) % total_rows
    key_pos = (key_start + lanes[None, None, :] + offset_col[:, None, None] - rotation) % total_rows
    return (query_pos // segment == key_pos // segment) & (key_pos <= query_pos)


def forward_tile(running, query_pack, key_pair, linked, score_scale):
    row_top, row_total, accumulated = running
    scores = (
        jnp.einsum("ahd,bhd->hab", query_pack, key_pair[0], preferred_element_type=jnp.float32)
        * score_scale
    )
    scores = jnp.where(linked, scores, NEGATIVE_FILL)
    new_top = jnp.maximum(row_top, jnp.max(scores, axis=2).T)
    weights = jnp.where(linked, jnp.exp(scores - new_top.T[:, :, None]), 0.0)
    factor = jnp.exp(row_top - new_top)
    row_total = row_total * factor + jnp.sum(weights, axis=2).T
    weights_high = weights.astype(jnp.bfloat16)
    weights_rest = (weights - weights_high.astype(jnp.float32)).astype(jnp.bfloat16)
    product = jnp.einsum(
        "hab,bhd->ahd", weights_high, key_pair[1], preferred_element_type=jnp.float32
    )
    product = product + jnp.einsum(
        "hab,bhd->ahd", weights_rest, key_pair[1], preferred_element_type=jnp.float32
    )
    accumulated = accumulated * factor[:, :, None] + product
    return (new_top, row_total, accumulated)


def tile_grads(query_side, key_pair, linked, score_scale):
    query_pack, grad_pack, log_pack, delta_pack = query_side
    scores = (
        jnp.einsum("ahd,bhd->hab", query_pack, key_pair[0], preferred_element_type=jnp.float32)
        * score_scale
    )
    scores = jnp.where(linked, scores, NEGATIVE_FILL)
    weights = jnp.where(linked, jnp.exp(scores - log_pack.T[:, :, None]), 0.0)
    prob_grad = jnp.einsum(
        "ahd,bhd->hab", grad_pack, key_pair[1], preferred_element_type=jnp.float32
    )
    score_grad = (weights * (prob_grad - delta_pack.T[:, :, None])).astype(jnp.bfloat16)
    return (weights.astype(jnp.bfloat16), score_grad)


def forward_relay(
    running, query_pack, key_pair, offset_col, stride, segment, relay_turns, score_scale
):
    row_count = query_pack.shape[0]
    tok_rows = row_count * stride
    axis_size = lax.axis_size("ctx")
    device_index = lax.axis_index("ctx")
    stored = (
        jnp.zeros((max(relay_turns, 1),) + key_pair[0].shape, key_pair[0].dtype),
        jnp.zeros((max(relay_turns, 1),) + key_pair[1].shape, key_pair[1].dtype),
    )

    def forward_turn_body(turn_num, carried):
        packet, running, stored = carried
        packet = jax.tree.map(
            lambda part, own: part.astype(own.dtype),
            passed_along(for_sending(packet), "ctx", 1),
            packet,
        )
        key_start = (device_index - turn_num) % axis_size * tok_rows
        linked = linked_pairs(
            offset_col, stride, segment, device_index * tok_rows, key_start, row_count
        )
        running = forward_tile(running, query_pack, packet, linked, score_scale)
        return (packet, running, stored)

    packet, running, stored = lax.fori_loop(
        1, relay_turns + 1, forward_turn_body, (key_pair, running, stored)
    )
    return (running, stored)


def keys_pass(query_side, key_pair, offset_col, stride, segment, relay_turns, score_scale):
    query_pack, grad_pack = (query_side[0], query_side[1])
    row_count = query_pack.shape[0]
    tok_rows = row_count * stride
    axis_size = lax.axis_size("ctx")
    device_index = lax.axis_index("ctx")
    own_start = device_index * tok_rows
    weights_low, score_grad = tile_grads(
        query_side,
        key_pair,
        linked_pairs(offset_col, stride, segment, own_start, own_start, row_count),
        score_scale,
    )
    level_q = jnp.einsum(
        "hab,bhd->ahd", score_grad, key_pair[0], preferred_element_type=jnp.float32
    )
    partial_value = (
        jnp.einsum("hab,ahd->bhd", score_grad, query_pack, preferred_element_type=jnp.float32),
        jnp.einsum("hab,ahd->bhd", weights_low, grad_pack, preferred_element_type=jnp.float32),
    )

    def keys_turn_body(turn_num, carried):
        packet, partial_value, level_q = carried
        packet = jax.tree.map(
            lambda part, own: part.astype(own.dtype),
            passed_along(for_sending(packet), "ctx", 1),
            packet,
        )
        partial_value = jax.tree.map(
            lambda part, own: part.astype(own.dtype),
            passed_along(for_sending(partial_value), "ctx", 1),
            partial_value,
        )
        key_start = (device_index - turn_num) % axis_size * tok_rows
        weights_low, score_grad = tile_grads(
            query_side,
            packet,
            linked_pairs(offset_col, stride, segment, own_start, key_start, row_count),
            score_scale,
        )
        level_q = level_q + jnp.einsum(
            "hab,bhd->ahd", score_grad, packet[0], preferred_element_type=jnp.float32
        )
        partial_value = (
            partial_value[0]
            + jnp.einsum(
                "hab,ahd->bhd", score_grad, query_pack, preferred_element_type=jnp.float32
            ),
            partial_value[1]
            + jnp.einsum(
                "hab,ahd->bhd", weights_low, grad_pack, preferred_element_type=jnp.float32
            ),
        )
        return (packet, partial_value, level_q)

    packet, partial_value, level_q = lax.fori_loop(
        1, relay_turns + 1, keys_turn_body, (key_pair, partial_value, level_q)
    )
    partial_value = (
        passed_along(partial_value[0].astype(jnp.bfloat16), "ctx", -relay_turns).astype(
            jnp.float32
        ),
        passed_along(partial_value[1].astype(jnp.bfloat16), "ctx", -relay_turns).astype(
            jnp.float32
        ),
    )
    return (level_q, partial_value[0], partial_value[1])


def local(queries, keys, values, out_grad, w_out, offsets):
    tok_rows = queries.shape[0]
    head_count = offsets.shape[0]
    head_width = queries.shape[1] // head_count
    axis_size = lax.axis_size("ctx")
    device_index = lax.axis_index("ctx")
    keys_seg = KEYS_SEG
    score_scale = 1.0 / math.sqrt(head_width)
    own_start = device_index * tok_rows
    query_rows = queries.reshape(tok_rows, head_count, head_width)
    key_rows = keys.reshape(tok_rows, head_count, head_width)
    value_rows = values.reshape(tok_rows, head_count, head_width)
    grad_out = jnp.einsum(
        "td,fd->tf",
        lax.all_gather(out_grad, "tp", axis=1, tiled=True),
        w_out,
        preferred_element_type=jnp.float32,
    )
    grad_rows = grad_out.astype(jnp.bfloat16).reshape(tok_rows, head_count, head_width)
    level_data = []
    for level_num in range(LEVELS):
        stride = 2**level_num
        segment = min(keys_seg * stride, tok_rows * axis_size)
        row_count = tok_rows // stride
        relay_turns = min(max(segment // tok_rows, 1), axis_size) - 1
        offset_col = offsets[:, level_num]
        pick = pick_table(offset_col, stride)
        query_pack = pack_rows(query_rows, pick)
        key_pair = (pack_rows(key_rows, pick), pack_rows(value_rows, pick))
        running = (
            jnp.full((row_count, head_count), NEGATIVE_FILL, jnp.float32),
            jnp.zeros((row_count, head_count), jnp.float32),
            jnp.zeros((row_count, head_count, head_width), jnp.float32),
        )
        linked = linked_pairs(offset_col, stride, segment, own_start, own_start, row_count)
        running = forward_tile(running, query_pack, key_pair, linked, score_scale)
        running, stored = forward_relay(
            running, query_pack, key_pair, offset_col, stride, segment, relay_turns, score_scale
        )
        level_data.append(
            (stride, segment, relay_turns, offset_col, pick, query_pack, key_pair, running, stored)
        )
    tops = [spread_rows(entry[7][0], entry[4], NEGATIVE_FILL) for entry in level_data]
    row_top = reduce(jnp.maximum, tops)
    row_total = jnp.zeros((tok_rows, head_count), jnp.float32)
    out_sum = jnp.zeros((tok_rows, head_count, head_width), jnp.float32)
    for entry, level_top in zip(level_data, tops):
        factor = jnp.exp(level_top - row_top)
        row_total = row_total + spread_rows(entry[7][1], entry[4], 0.0) * factor
        out_sum = out_sum + spread_rows(entry[7][2], entry[4], 0.0) * factor[:, :, None]
    log_total = row_top + jnp.log(row_total)
    attn_out = out_sum / row_total[:, :, None]
    delta_rows = jnp.sum(grad_rows.astype(jnp.float32) * attn_out, axis=2)
    grad_q = jnp.zeros((tok_rows, head_count, head_width), jnp.float32)
    grad_k = jnp.zeros((tok_rows, head_count, head_width), jnp.float32)
    grad_v = jnp.zeros((tok_rows, head_count, head_width), jnp.float32)
    for (
        stride,
        segment,
        relay_turns,
        offset_col,
        pick,
        query_pack,
        key_pair,
        running,
        stored,
    ) in level_data:
        query_side = (
            query_pack,
            pack_rows(grad_rows, pick),
            pack_rows(log_total, pick),
            pack_rows(delta_rows, pick),
        )
        level_q, level_k, level_v = keys_pass(
            query_side, key_pair, offset_col, stride, segment, relay_turns, score_scale
        )
        grad_q = grad_q + spread_rows(level_q, pick, 0.0)
        grad_k = grad_k + spread_rows(level_k, pick, 0.0)
        grad_v = grad_v + spread_rows(level_v, pick, 0.0)
    flat_width = head_count * head_width
    return (
        (grad_q * score_scale).reshape(tok_rows, flat_width).astype(jnp.bfloat16),
        (grad_k * score_scale).reshape(tok_rows, flat_width).astype(jnp.bfloat16),
        grad_v.reshape(tok_rows, flat_width).astype(jnp.bfloat16),
    )


def solution(mesh):
    return jax.shard_map(
        local,
        mesh=mesh,
        in_specs=(
            P("ctx", "tp"),
            P("ctx", "tp"),
            P("ctx", "tp"),
            P("ctx", "tp"),
            P("tp", None),
            P("tp", None),
        ),
        out_specs=(P("ctx", "tp"), P("ctx", "tp"), P("ctx", "tp")),
        check_vma=False,
    )
```

profile of v0, /device:TPU:8, one launch (start us, length us, event | category | flops | bytes accessed | tf_op | source)
XLA Modules:
  0.0 601.4 jit_solution(17598615191669970776)
XLA Ops:
  20.9 12.5 %all-gather.2.cloned.1.call-done = bf16[256,4096]{1,0:T(8,128)(2,1)} async-done(((bf16[256,1024]{1,0:T(8,128)(2,1)}), bf16[256,4096]{1,0:T(8,128)(2,1)}) %all-gather.2.cloned.1.call-update) | async-done | bytes 2097168 | tf_op jit(solution)/shard_map/all_gather | solution.py:213
  33.4 4.1 convolution_convert_fusion
  47.0 2.8 select_reduce_fusion.1
  54.2 2.7 fusion.105
  59.7 55.5 %while.144 = (s32[]{:T(128)}, bf16[256,4,128]{2,0,1:T(8,128)(2,1)}, bf16[256,4,128]{2,0,1:T(8,128)(2,1)}, f32[256,4]{0,1:T(4,128)S(1)}, f32[256,4]{0,1:T(4,128)S...) while((s32[]{:T(128)}, bf16[256,4,128]{2,0,1:T(8,128)(2,1)}, ...), condition=%wide.region_5.6_spmd, body=%wide.region_2.5_spmd.sunk | while | flops 208857616 | bytes 10641786 | solution.py:124
  63.4 6.6 %collective-permute-done = bf16[256,4,128]{2,0,1:T(8,128)(2,1)S(1)} collective-permute-done((bf16[256,4,128]{2,0,1:T(8,128)(2,1)}, bf16[256,4,128]{2,0,1:T(8,128)(2,1)S(1)}, u32[]{:S(2)}, u32[]{:S(2)}) %collective-permute-start) | collective-permute-done | bytes 262176 | tf_op jit(solution)/shard_map/while/body/eval_jaxpr/ppermute | solution.py:27
  71.4 3.5 collective-permute-done.1
  82.8 6.7 %collective-permute-done = bf16[256,4,128]{2,0,1:T(8,128)(2,1)S(1)} collective-permute-done((bf16[256,4,128]{2,0,1:T(8,128)(2,1)}, bf16[256,4,128]{2,0,1:T(8,128)(2,1)S(1)}, u32[]{:S(2)}, u32[]{:S(2)}) %collective-permute-start) | collective-permute-done | bytes 262176 | tf_op jit(solution)/shard_map/while/body/eval_jaxpr/ppermute | solution.py:27
  90.9 2.6 collective-permute-done.1
  97.6 2.9 collective-permute-start.1
  101.3 6.7 %collective-permute-done = bf16[256,4,128]{2,0,1:T(8,128)(2,1)S(1)} collective-permute-done((bf16[256,4,128]{2,0,1:T(8,128)(2,1)}, bf16[256,4,128]{2,0,1:T(8,128)(2,1)S(1)}, u32[]{:S(2)}, u32[]{:S(2)}) %collective-permute-start) | collective-permute-done | bytes 262176 | tf_op jit(solution)/shard_map/while/body/eval_jaxpr/ppermute | solution.py:27
  115.9 59.2 %while.146 = (s32[]{:T(128)}, bf16[64,4,128]{2,0,1:T(8,128)(2,1)S(1)}, bf16[64,4,128]{2,0,1:T(8,128)(2,1)S(1)}, f32[64,4]{0,1:T(4,128)S(1)}, f32[64,4]{0,1:T(4,1...) while((s32[]{:T(128)}, ...), condition=%wide.region_23.24_spmd, body=%wide.region_20.23_spmd.sunk | while | flops 13138703 | bytes 1874298 | solution.py:124
  116.0 3.0 collective-permute-start.5
  126.3 3.0 collective-permute-done.4
  130.9 4.1 collective-permute-start.5
  140.9 3.4 collective-permute-start.5
  149.3 3.2 collective-permute-start.5
  153.2 2.8 collective-permute-done.4
  160.9 4.3 collective-permute-done.4
  166.6 2.6 collective-permute-start.5
  169.9 3.1 collective-permute-done.4
  178.1 79.2 %while.145 = (s32[]{:T(128)}, bf16[128,4,128]{2,0,1:T(8,128)(2,1)S(1)}, bf16[128,4,128]{2,0,1:T(8,128)(2,1)S(1)}, f32[128,4]{0,1:T(4,128)S(1)}, f32[128,4]{0,1:T...) while((s32[]{:T(128)}, ...), condition=%wide.region_14.15_spmd, body=%wide.region_11.14_spmd.sunk | while | flops 52327952 | bytes 4272506 | solution.py:124
  178.1 3.6 collective-permute-start.3
  182.4 5.1 collective-permute-done.2
  192.4 7.5 %collective-permute-done.2 = bf16[128,4,128]{2,0,1:T(8,128)(2,1)S(1)} collective-permute-done((bf16[128,4,128]{2,0,1:T(8,128)(2,1)S(1)}, bf16[128,4,128]{2,0,1:T(8,128)(2,1)S(1)}, u32[]{:S(2)}, u32[]{:S(2)}) %collective-permute-start.2) | collective-permute-done | bytes 131104 | tf_op jit(solution)/shard_map/while/body/eval_jaxpr/ppermute | solution.py:27
  204.0 6.2 %collective-permute-done.2 = bf16[128,4,128]{2,0,1:T(8,128)(2,1)S(1)} collective-permute-done((bf16[128,4,128]{2,0,1:T(8,128)(2,1)S(1)}, bf16[128,4,128]{2,0,1:T(8,128)(2,1)S(1)}, u32[]{:S(2)}, u32[]{:S(2)}) %collective-permute-start.2) | collective-permute-done | bytes 131104 | tf_op jit(solution)/shard_map/while/body/eval_jaxpr/ppermute | solution.py:27
  215.1 5.9 collective-permute-done.2
  226.4 5.5 collective-permute-done.2
  235.2 2.7 collective-permute-start.3
  238.7 4.2 collective-permute-done.2
  248.5 5.3 collective-permute-done.2
  297.7 80.9 %while.147 = (s32[]{:T(128)}, bf16[256,4,128]{2,0,1:T(8,128)(2,1)S(1)}, bf16[256,4,128]{2,0,1:T(8,128)(2,1)S(1)}, bf16[256,4,128]{2,0,1:T(8,128)(2,1)}, bf16[256...) while((s32[]{:T(128)}, ...), condition=%wide.region_26.27_spmd, body=%wide.region_25.26_spmd.sunk | while | flops 339403264 | bytes 13939170 | solution.py:185
  301.6 4.5 collective-permute-start.9
  306.8 2.9 collective-permute-done.6
  311.4 3.9 collective-permute-done.7
  316.0 4.9 collective-permute-done.8
  322.0 3.1 collective-permute-done.9
  328.0 3.3 collective-permute-start.9
  332.0 5.8 collective-permute-done.6
  339.5 3.9 collective-permute-done.7
  344.0 5.0 collective-permute-done.8
  353.6 4.0 collective-permute-start.9
  358.4 6.4 %collective-permute-done.6 = bf16[256,4,128]{2,0,1:T(8,128)(2,1)S(1)} collective-permute-done((bf16[256,4,128]{2,0,1:T(8,128)(2,1)S(1)}, bf16[256,4,128]{2,0,1:T(8,128)(2,1)S(1)}, u32[]{:S(2)}, u32[]{:S(2)}) %collective-permute-start.6) | collective-permute-done | bytes 262176 | tf_op jit(solution)/shard_map/while/body/eval_jaxpr/ppermute | solution.py:27
  366.5 3.9 collective-permute-done.7
  371.0 3.7 collective-permute-done.8
  379.7 4.7 collective-permute-start.18
  385.5 109.8 %while.148 = (s32[]{:T(128)}, bf16[128,4,128]{2,0,1:T(8,128)(2,1)}, bf16[128,4,128]{2,0,1:T(8,128)(2,1)S(1)}, bf16[128,4,128]{2,0,1:T(8,128)(2,1)}, bf16[128,4,1...) while((s32[]{:T(128)}, bf16[128,4,128]{2,0,1:T(8,128)(2,1)}, ...), condition=%wide.region_31.32_spmd, body=%wide.region_30.31_spmd.sunk | while | flops 85094928 | bytes 5790178 | solution.py:185
  388.6 4.6 collective-permute-done.10
  401.4 2.9 collective-permute-start.11
  419.9 2.7 collective-permute-start.13
  434.9 3.3 collective-permute-start.13
  452.4 3.3 collective-permute-start.13
  469.7 2.6 collective-permute-start.13
  479.8 5.1 collective-permute-start.11
  487.3 2.6 collective-permute-start.13
  495.4 76.9 %while.149 = (s32[]{:T(128)}, bf16[64,4,128]{2,0,1:T(8,128)(2,1)S(1)}, bf16[64,4,128]{2,0,1:T(8,128)(2,1)S(1)}, bf16[64,4,128]{2,0,1:T(8,128)(2,1)S(1)}, bf16[64...) while((s32[]{:T(128)}, ...), condition=%wide.region_36.37_spmd, body=%wide.region_35.36_spmd.sunk | while | flops 21395728 | bytes 2600418 | solution.py:185
  496.6 2.7 collective-permute-start.15
  500.8 3.2 collective-permute-start.16
  508.6 3.4 collective-permute-start.15
  517.5 3.0 collective-permute-done.16
  530.8 2.6 collective-permute-start.15
  542.8 3.4 collective-permute-start.15
  546.3 2.6 collective-permute-start.16
  577.3 4.5 collective-permute-done.23
  (874 shorter events, 344.7 us)
Async XLA Ops:
  7.2 26.2 %all-gather.2.cloned.1.call-start = ((), (), s32[]{:S(2)}) async-start(), calls=%async_computation | async-start | bytes 2621440 | tf_op jit(solution)/shard_map/all_gather | solution.py:213
  59.7 10.3 %collective-permute-start = (bf16[256,4,128]{2,0,1:T(8,128)(2,1)}, bf16[256,4,128]{2,0,1:T(8,128)(2,1)S(1)}, u32[]{:S(2)}, u32[]{:S(2)}) collective-permute-start(bf16[256,4,128]{2,0,1:T(8,128)(2,1)} %get-tuple-element.3054), channel_id=1, source_target_pairs={{28,0},{0,4},{4,8},{8,12},{12,16},{16,20},{20,24},{24,28},{29,1},{... | collective-permute-start | bytes 786440 | tf_op jit(solution)/shard_map/while/body/eval_jaxpr/ppermute | solution.py:27
  61.2 13.7 %collective-permute-start.1 = (bf16[256,4,128]{2,0,1:T(8,128)(2,1)}, bf16[256,4,128]{2,0,1:T(8,128)(2,1)S(1)}, u32[]{:S(2)}, u32[]{:S(2)}) collective-permute-start(bf16[256,4,128]{2,0,1:T(8,128)(2,1)} %get-tuple-element.3055), channel_id=1, source_target_pairs={{28,0},{0,4},{4,8},{8,12},{12,16},{16,20},{20,24},{24,28},{29,1},{... | collective-permute-start | bytes 786440 | tf_op jit(solution)/shard_map/while/body/eval_jaxpr/ppermute | solution.py:27
  79.0 10.4 %collective-permute-start = (bf16[256,4,128]{2,0,1:T(8,128)(2,1)}, bf16[256,4,128]{2,0,1:T(8,128)(2,1)S(1)}, u32[]{:S(2)}, u32[]{:S(2)}) collective-permute-start(bf16[256,4,128]{2,0,1:T(8,128)(2,1)} %get-tuple-element.3054), channel_id=1, source_target_pairs={{28,0},{0,4},{4,8},{8,12},{12,16},{16,20},{20,24},{24,28},{29,1},{... | collective-permute-start | bytes 786440 | tf_op jit(solution)/shard_map/while/body/eval_jaxpr/ppermute | solution.py:27
  79.7 13.8 %collective-permute-start.1 = (bf16[256,4,128]{2,0,1:T(8,128)(2,1)}, bf16[256,4,128]{2,0,1:T(8,128)(2,1)S(1)}, u32[]{:S(2)}, u32[]{:S(2)}) collective-permute-start(bf16[256,4,128]{2,0,1:T(8,128)(2,1)} %get-tuple-element.3055), channel_id=1, source_target_pairs={{28,0},{0,4},{4,8},{8,12},{12,16},{16,20},{20,24},{24,28},{29,1},{... | collective-permute-start | bytes 786440 | tf_op jit(solution)/shard_map/while/body/eval_jaxpr/ppermute | solution.py:27
  97.6 10.4 %collective-permute-start = (bf16[256,4,128]{2,0,1:T(8,128)(2,1)}, bf16[256,4,128]{2,0,1:T(8,128)(2,1)S(1)}, u32[]{:S(2)}, u32[]{:S(2)}) collective-permute-start(bf16[256,4,128]{2,0,1:T(8,128)(2,1)} %get-tuple-element.3054), channel_id=1, source_target_pairs={{28,0},{0,4},{4,8},{8,12},{12,16},{16,20},{20,24},{24,28},{29,1},{... | collective-permute-start | bytes 786440 | tf_op jit(solution)/shard_map/while/body/eval_jaxpr/ppermute | solution.py:27
  97.6 13.4 %collective-permute-start.1 = (bf16[256,4,128]{2,0,1:T(8,128)(2,1)}, bf16[256,4,128]{2,0,1:T(8,128)(2,1)S(1)}, u32[]{:S(2)}, u32[]{:S(2)}) collective-permute-start(bf16[256,4,128]{2,0,1:T(8,128)(2,1)} %get-tuple-element.3055), channel_id=1, source_target_pairs={{28,0},{0,4},{4,8},{8,12},{12,16},{16,20},{20,24},{24,28},{29,1},{... | collective-permute-start | bytes 786440 | tf_op jit(solution)/shard_map/while/body/eval_jaxpr/ppermute | solution.py:27
  147.9 8.0 %collective-permute-start.4 = (bf16[64,4,128]{2,0,1:T(8,128)(2,1)S(1)}, bf16[64,4,128]{2,0,1:T(8,128)(2,1)S(1)}, u32[]{:S(2)}, u32[]{:S(2)}) collective-permute-start(bf16[64,4,128]{2,0,1:T(8,128)(2,1)S(1)} %get-tuple-element.3009), channel_id=1, source_target_pairs={{28,0},{0,4},{4,8},{8,12},{12,16},{16,20},{20,24},{24,28},{29,1},{... | collective-permute-start | bytes 196616 | tf_op jit(solution)/shard_map/while/body/eval_jaxpr/ppermute | solution.py:27
  149.3 7.8 %collective-permute-start.5 = (bf16[64,4,128]{2,0,1:T(8,128)(2,1)S(1)}, bf16[64,4,128]{2,0,1:T(8,128)(2,1)S(1)}, u32[]{:S(2)}, u32[]{:S(2)}) collective-permute-start(bf16[64,4,128]{2,0,1:T(8,128)(2,1)S(1)} %get-tuple-element.3010), channel_id=1, source_target_pairs={{28,0},{0,4},{4,8},{8,12},{12,16},{16,20},{20,24},{24,28},{29,1},{... | collective-permute-start | bytes 196616 | tf_op jit(solution)/shard_map/while/body/eval_jaxpr/ppermute | solution.py:27
  157.9 8.0 %collective-permute-start.5 = (bf16[64,4,128]{2,0,1:T(8,128)(2,1)S(1)}, bf16[64,4,128]{2,0,1:T(8,128)(2,1)S(1)}, u32[]{:S(2)}, u32[]{:S(2)}) collective-permute-start(bf16[64,4,128]{2,0,1:T(8,128)(2,1)S(1)} %get-tuple-element.3010), channel_id=1, source_target_pairs={{28,0},{0,4},{4,8},{8,12},{12,16},{16,20},{20,24},{24,28},{29,1},{... | collective-permute-start | bytes 196616 | tf_op jit(solution)/shard_map/while/body/eval_jaxpr/ppermute | solution.py:27
  166.6 7.8 %collective-permute-start.5 = (bf16[64,4,128]{2,0,1:T(8,128)(2,1)S(1)}, bf16[64,4,128]{2,0,1:T(8,128)(2,1)S(1)}, u32[]{:S(2)}, u32[]{:S(2)}) collective-permute-start(bf16[64,4,128]{2,0,1:T(8,128)(2,1)S(1)} %get-tuple-element.3010), channel_id=1, source_target_pairs={{28,0},{0,4},{4,8},{8,12},{12,16},{16,20},{20,24},{24,28},{29,1},{... | collective-permute-start | bytes 196616 | tf_op jit(solution)/shard_map/while/body/eval_jaxpr/ppermute | solution.py:27
  178.1 9.4 %collective-permute-start.2 = (bf16[128,4,128]{2,0,1:T(8,128)(2,1)S(1)}, bf16[128,4,128]{2,0,1:T(8,128)(2,1)S(1)}, u32[]{:S(2)}, u32[]{:S(2)}) collective-permute-start(bf16[128,4,128]{2,0,1:T(8,128)(2,1)S(1)} %get-tuple-element.2964), channel_id=1, source_target_pairs={{28,0},{0,4},{4,8},{8,12},{12,16},{16,20},{20,24},{24,28},{29,1},{... | collective-permute-start | bytes 393224 | tf_op jit(solution)/shard_map/while/body/eval_jaxpr/ppermute | solution.py:27
  178.1 11.2 %collective-permute-start.3 = (bf16[128,4,128]{2,0,1:T(8,128)(2,1)S(1)}, bf16[128,4,128]{2,0,1:T(8,128)(2,1)S(1)}, u32[]{:S(2)}, u32[]{:S(2)}) collective-permute-start(bf16[128,4,128]{2,0,1:T(8,128)(2,1)S(1)} %get-tuple-element.2965), channel_id=1, source_target_pairs={{28,0},{0,4},{4,8},{8,12},{12,16},{16,20},{20,24},{24,28},{29,1},{... | collective-permute-start | bytes 393224 | tf_op jit(solution)/shard_map/while/body/eval_jaxpr/ppermute | solution.py:27
  190.8 9.1 %collective-permute-start.2 = (bf16[128,4,128]{2,0,1:T(8,128)(2,1)S(1)}, bf16[128,4,128]{2,0,1:T(8,128)(2,1)S(1)}, u32[]{:S(2)}, u32[]{:S(2)}) collective-permute-start(bf16[128,4,128]{2,0,1:T(8,128)(2,1)S(1)} %get-tuple-element.2964), channel_id=1, source_target_pairs={{28,0},{0,4},{4,8},{8,12},{12,16},{16,20},{20,24},{24,28},{29,1},{... | collective-permute-start | bytes 393224 | tf_op jit(solution)/shard_map/while/body/eval_jaxpr/ppermute | solution.py:27
  190.8 10.9 %collective-permute-start.3 = (bf16[128,4,128]{2,0,1:T(8,128)(2,1)S(1)}, bf16[128,4,128]{2,0,1:T(8,128)(2,1)S(1)}, u32[]{:S(2)}, u32[]{:S(2)}) collective-permute-start(bf16[128,4,128]{2,0,1:T(8,128)(2,1)S(1)} %get-tuple-element.2965), channel_id=1, source_target_pairs={{28,0},{0,4},{4,8},{8,12},{12,16},{16,20},{20,24},{24,28},{29,1},{... | collective-permute-start | bytes 393224 | tf_op jit(solution)/shard_map/while/body/eval_jaxpr/ppermute | solution.py:27
  203.2 8.9 %collective-permute-start.3 = (bf16[128,4,128]{2,0,1:T(8,128)(2,1)S(1)}, bf16[128,4,128]{2,0,1:T(8,128)(2,1)S(1)}, u32[]{:S(2)}, u32[]{:S(2)}) collective-permute-start(bf16[128,4,128]{2,0,1:T(8,128)(2,1)S(1)} %get-tuple-element.2965), channel_id=1, source_target_pairs={{28,0},{0,4},{4,8},{8,12},{12,16},{16,20},{20,24},{24,28},{29,1},{... | collective-permute-start | bytes 393224 | tf_op jit(solution)/shard_map/while/body/eval_jaxpr/ppermute | solution.py:27
  213.6 9.2 %collective-permute-start.3 = (bf16[128,4,128]{2,0,1:T(8,128)(2,1)S(1)}, bf16[128,4,128]{2,0,1:T(8,128)(2,1)S(1)}, u32[]{:S(2)}, u32[]{:S(2)}) collective-permute-start(bf16[128,4,128]{2,0,1:T(8,128)(2,1)S(1)} %get-tuple-element.2965), channel_id=1, source_target_pairs={{28,0},{0,4},{4,8},{8,12},{12,16},{16,20},{20,24},{24,28},{29,1},{... | collective-permute-start | bytes 393224 | tf_op jit(solution)/shard_map/while/body/eval_jaxpr/ppermute | solution.py:27
  224.3 9.5 %collective-permute-start.3 = (bf16[128,4,128]{2,0,1:T(8,128)(2,1)S(1)}, bf16[128,4,128]{2,0,1:T(8,128)(2,1)S(1)}, u32[]{:S(2)}, u32[]{:S(2)}) collective-permute-start(bf16[128,4,128]{2,0,1:T(8,128)(2,1)S(1)} %get-tuple-element.2965), channel_id=1, source_target_pairs={{28,0},{0,4},{4,8},{8,12},{12,16},{16,20},{20,24},{24,28},{29,1},{... | collective-permute-start | bytes 393224 | tf_op jit(solution)/shard_map/while/body/eval_jaxpr/ppermute | solution.py:27
  235.2 9.5 %collective-permute-start.3 = (bf16[128,4,128]{2,0,1:T(8,128)(2,1)S(1)}, bf16[128,4,128]{2,0,1:T(8,128)(2,1)S(1)}, u32[]{:S(2)}, u32[]{:S(2)}) collective-permute-start(bf16[128,4,128]{2,0,1:T(8,128)(2,1)S(1)} %get-tuple-element.2965), channel_id=1, source_target_pairs={{28,0},{0,4},{4,8},{8,12},{12,16},{16,20},{20,24},{24,28},{29,1},{... | collective-permute-start | bytes 393224 | tf_op jit(solution)/shard_map/while/body/eval_jaxpr/ppermute | solution.py:27
  246.2 9.5 %collective-permute-start.3 = (bf16[128,4,128]{2,0,1:T(8,128)(2,1)S(1)}, bf16[128,4,128]{2,0,1:T(8,128)(2,1)S(1)}, u32[]{:S(2)}, u32[]{:S(2)}) collective-permute-start(bf16[128,4,128]{2,0,1:T(8,128)(2,1)S(1)} %get-tuple-element.2965), channel_id=1, source_target_pairs={{28,0},{0,4},{4,8},{8,12},{12,16},{16,20},{20,24},{24,28},{29,1},{... | collective-permute-start | bytes 393224 | tf_op jit(solution)/shard_map/while/body/eval_jaxpr/ppermute | solution.py:27
  297.7 12.0 %collective-permute-start.6 = (bf16[256,4,128]{2,0,1:T(8,128)(2,1)S(1)}, bf16[256,4,128]{2,0,1:T(8,128)(2,1)S(1)}, u32[]{:S(2)}, u32[]{:S(2)}) collective-permute-start(bf16[256,4,128]{2,0,1:T(8,128)(2,1)S(1)} %get-tuple-element.3156), channel_id=1, source_target_pairs={{28,0},{0,4},{4,8},{8,12},{12,16},{16,20},{20,24},{24,28},{29,1},{... | collective-permute-start | bytes 786440 | tf_op jit(solution)/shard_map/while/body/eval_jaxpr/ppermute | solution.py:27
  297.8 17.5 %collective-permute-start.7 = (bf16[256,4,128]{2,0,1:T(8,128)(2,1)S(1)}, bf16[256,4,128]{2,0,1:T(8,128)(2,1)S(1)}, u32[]{:S(2)}, u32[]{:S(2)}) collective-permute-start(bf16[256,4,128]{2,0,1:T(8,128)(2,1)S(1)} %get-tuple-element.3157), channel_id=1, source_target_pairs={{28,0},{0,4},{4,8},{8,12},{12,16},{16,20},{20,24},{24,28},{29,1},{... | collective-permute-start | bytes 786440 | tf_op jit(solution)/shard_map/while/body/eval_jaxpr/ppermute | solution.py:27
  299.2 21.7 %collective-permute-start.8 = (bf16[256,4,128]{2,0,1:T(8,128)(2,1)}, bf16[256,4,128]{2,0,1:T(8,128)(2,1)S(1)}, u32[]{:S(2)}, u32[]{:S(2)}) collective-permute-start(bf16[256,4,128]{2,0,1:T(8,128)(2,1)} %get-tuple-element.3158), channel_id=1, source_target_pairs={{28,0},{0,4},{4,8},{8,12},{12,16},{16,20},{20,24},{24,28},{29,1},{... | collective-permute-start | bytes 786440 | tf_op jit(solution)/shard_map/while/body/eval_jaxpr/ppermute | solution.py:27
  301.6 23.5 %collective-permute-start.9 = (bf16[256,4,128]{2,0,1:T(8,128)(2,1)}, bf16[256,4,128]{2,0,1:T(8,128)(2,1)S(1)}, u32[]{:S(2)}, u32[]{:S(2)}) collective-permute-start(bf16[256,4,128]{2,0,1:T(8,128)(2,1)} %get-tuple-element.3159), channel_id=1, source_target_pairs={{28,0},{0,4},{4,8},{8,12},{12,16},{16,20},{20,24},{24,28},{29,1},{... | collective-permute-start | bytes 786440 | tf_op jit(solution)/shard_map/while/body/eval_jaxpr/ppermute | solution.py:27
  326.1 11.6 %collective-permute-start.6 = (bf16[256,4,128]{2,0,1:T(8,128)(2,1)S(1)}, bf16[256,4,128]{2,0,1:T(8,128)(2,1)S(1)}, u32[]{:S(2)}, u32[]{:S(2)}) collective-permute-start(bf16[256,4,128]{2,0,1:T(8,128)(2,1)S(1)} %get-tuple-element.3156), channel_id=1, source_target_pairs={{28,0},{0,4},{4,8},{8,12},{12,16},{16,20},{20,24},{24,28},{29,1},{... | collective-permute-start | bytes 786440 | tf_op jit(solution)/shard_map/while/body/eval_jaxpr/ppermute | solution.py:27
  326.1 17.3 %collective-permute-start.7 = (bf16[256,4,128]{2,0,1:T(8,128)(2,1)S(1)}, bf16[256,4,128]{2,0,1:T(8,128)(2,1)S(1)}, u32[]{:S(2)}, u32[]{:S(2)}) collective-permute-start(bf16[256,4,128]{2,0,1:T(8,128)(2,1)S(1)} %get-tuple-element.3157), channel_id=1, source_target_pairs={{28,0},{0,4},{4,8},{8,12},{12,16},{16,20},{20,24},{24,28},{29,1},{... | collective-permute-start | bytes 786440 | tf_op jit(solution)/shard_map/while/body/eval_jaxpr/ppermute | solution.py:27
  326.1 22.9 %collective-permute-start.8 = (bf16[256,4,128]{2,0,1:T(8,128)(2,1)}, bf16[256,4,128]{2,0,1:T(8,128)(2,1)S(1)}, u32[]{:S(2)}, u32[]{:S(2)}) collective-permute-start(bf16[256,4,128]{2,0,1:T(8,128)(2,1)} %get-tuple-element.3158), channel_id=1, source_target_pairs={{28,0},{0,4},{4,8},{8,12},{12,16},{16,20},{20,24},{24,28},{29,1},{... | collective-permute-start | bytes 786440 | tf_op jit(solution)/shard_map/while/body/eval_jaxpr/ppermute | solution.py:27
  328.0 24.2 %collective-permute-start.9 = (bf16[256,4,128]{2,0,1:T(8,128)(2,1)}, bf16[256,4,128]{2,0,1:T(8,128)(2,1)S(1)}, u32[]{:S(2)}, u32[]{:S(2)}) collective-permute-start(bf16[256,4,128]{2,0,1:T(8,128)(2,1)} %get-tuple-element.3159), channel_id=1, source_target_pairs={{28,0},{0,4},{4,8},{8,12},{12,16},{16,20},{20,24},{24,28},{29,1},{... | collective-permute-start | bytes 786440 | tf_op jit(solution)/shard_map/while/body/eval_jaxpr/ppermute | solution.py:27
  353.3 11.5 %collective-permute-start.6 = (bf16[256,4,128]{2,0,1:T(8,128)(2,1)S(1)}, bf16[256,4,128]{2,0,1:T(8,128)(2,1)S(1)}, u32[]{:S(2)}, u32[]{:S(2)}) collective-permute-start(bf16[256,4,128]{2,0,1:T(8,128)(2,1)S(1)} %get-tuple-element.3156), channel_id=1, source_target_pairs={{28,0},{0,4},{4,8},{8,12},{12,16},{16,20},{20,24},{24,28},{29,1},{... | collective-permute-start | bytes 786440 | tf_op jit(solution)/shard_map/while/body/eval_jaxpr/ppermute | solution.py:27
  353.3 17.1 %collective-permute-start.7 = (bf16[256,4,128]{2,0,1:T(8,128)(2,1)S(1)}, bf16[256,4,128]{2,0,1:T(8,128)(2,1)S(1)}, u32[]{:S(2)}, u32[]{:S(2)}) collective-permute-start(bf16[256,4,128]{2,0,1:T(8,128)(2,1)S(1)} %get-tuple-element.3157), channel_id=1, source_target_pairs={{28,0},{0,4},{4,8},{8,12},{12,16},{16,20},{20,24},{24,28},{29,1},{... | collective-permute-start | bytes 786440 | tf_op jit(solution)/shard_map/while/body/eval_jaxpr/ppermute | solution.py:27
  353.3 21.5 %collective-permute-start.8 = (bf16[256,4,128]{2,0,1:T(8,128)(2,1)}, bf16[256,4,128]{2,0,1:T(8,128)(2,1)S(1)}, u32[]{:S(2)}, u32[]{:S(2)}) collective-permute-start(bf16[256,4,128]{2,0,1:T(8,128)(2,1)} %get-tuple-element.3158), channel_id=1, source_target_pairs={{28,0},{0,4},{4,8},{8,12},{12,16},{16,20},{20,24},{24,28},{29,1},{... | collective-permute-start | bytes 786440 | tf_op jit(solution)/shard_map/while/body/eval_jaxpr/ppermute | solution.py:27
  353.6 23.9 %collective-permute-start.9 = (bf16[256,4,128]{2,0,1:T(8,128)(2,1)}, bf16[256,4,128]{2,0,1:T(8,128)(2,1)S(1)}, u32[]{:S(2)}, u32[]{:S(2)}) collective-permute-start(bf16[256,4,128]{2,0,1:T(8,128)(2,1)} %get-tuple-element.3159), channel_id=1, source_target_pairs={{28,0},{0,4},{4,8},{8,12},{12,16},{16,20},{20,24},{24,28},{29,1},{... | collective-permute-start | bytes 786440 | tf_op jit(solution)/shard_map/while/body/eval_jaxpr/ppermute | solution.py:27
  379.7 208.3 %collective-permute-start.18 = (bf16[256,4,128]{0,2,1:T(8,128)(2,1)S(1)}, bf16[256,4,128]{0,2,1:T(8,128)(2,1)}, u32[]{:S(2)}, u32[]{:S(2)}) collective-permute-start(bf16[256,4,128]{0,2,1:T(8,128)(2,1)S(1)} %copy.528), channel_id=1, source_target_pairs={{12,0},{16,4},{20,8},{24,12},{28,16},{0,20},{4,24},{8,28},{13,1},{... | collective-permute-start | bytes 786440 | tf_op jit(solution)/shard_map/ppermute | solution.py:27
  387.7 8.3 %collective-permute-start.11 = (bf16[128,4,128]{2,0,1:T(8,128)(2,1)S(1)}, bf16[128,4,128]{2,0,1:T(8,128)(2,1)S(1)}, u32[]{:S(2)}, u32[]{:S(2)}) collective-permute-start(bf16[128,4,128]{2,0,1:T(8,128)(2,1)S(1)} %get-tuple-element.3211), channel_id=1, source_target_pairs={{28,0},{0,4},{4,8},{8,12},{12,16},{16,20},{20,24},{24,28},{29,1},{... | collective-permute-start | bytes 393224 | tf_op jit(solution)/shard_map/while/body/eval_jaxpr/ppermute | solution.py:27
  387.8 11.0 %collective-permute-start.12 = (bf16[128,4,128]{2,0,1:T(8,128)(2,1)}, bf16[128,4,128]{2,0,1:T(8,128)(2,1)S(1)}, u32[]{:S(2)}, u32[]{:S(2)}) collective-permute-start(bf16[128,4,128]{2,0,1:T(8,128)(2,1)} %get-tuple-element.3212), channel_id=1, source_target_pairs={{28,0},{0,4},{4,8},{8,12},{12,16},{16,20},{20,24},{24,28},{29,1},{... | collective-permute-start | bytes 393224 | tf_op jit(solution)/shard_map/while/body/eval_jaxpr/ppermute | solution.py:27
  387.8 12.7 %collective-permute-start.13 = (bf16[128,4,128]{2,0,1:T(8,128)(2,1)}, bf16[128,4,128]{2,0,1:T(8,128)(2,1)S(1)}, u32[]{:S(2)}, u32[]{:S(2)}) collective-permute-start(bf16[128,4,128]{2,0,1:T(8,128)(2,1)} %get-tuple-element.3213), channel_id=1, source_target_pairs={{28,0},{0,4},{4,8},{8,12},{12,16},{16,20},{20,24},{24,28},{29,1},{... | collective-permute-start | bytes 393224 | tf_op jit(solution)/shard_map/while/body/eval_jaxpr/ppermute | solution.py:27
  401.4 10.3 %collective-permute-start.11 = (bf16[128,4,128]{2,0,1:T(8,128)(2,1)S(1)}, bf16[128,4,128]{2,0,1:T(8,128)(2,1)S(1)}, u32[]{:S(2)}, u32[]{:S(2)}) collective-permute-start(bf16[128,4,128]{2,0,1:T(8,128)(2,1)S(1)} %get-tuple-element.3211), channel_id=1, source_target_pairs={{28,0},{0,4},{4,8},{8,12},{12,16},{16,20},{20,24},{24,28},{29,1},{... | collective-permute-start | bytes 393224 | tf_op jit(solution)/shard_map/while/body/eval_jaxpr/ppermute | solution.py:27
  404.3 10.1 %collective-permute-start.12 = (bf16[128,4,128]{2,0,1:T(8,128)(2,1)}, bf16[128,4,128]{2,0,1:T(8,128)(2,1)S(1)}, u32[]{:S(2)}, u32[]{:S(2)}) collective-permute-start(bf16[128,4,128]{2,0,1:T(8,128)(2,1)} %get-tuple-element.3212), channel_id=1, source_target_pairs={{28,0},{0,4},{4,8},{8,12},{12,16},{16,20},{20,24},{24,28},{29,1},{... | collective-permute-start | bytes 393224 | tf_op jit(solution)/shard_map/while/body/eval_jaxpr/ppermute | solution.py:27
  405.4 11.1 %collective-permute-start.13 = (bf16[128,4,128]{2,0,1:T(8,128)(2,1)}, bf16[128,4,128]{2,0,1:T(8,128)(2,1)S(1)}, u32[]{:S(2)}, u32[]{:S(2)}) collective-permute-start(bf16[128,4,128]{2,0,1:T(8,128)(2,1)} %get-tuple-element.3213), channel_id=1, source_target_pairs={{28,0},{0,4},{4,8},{8,12},{12,16},{16,20},{20,24},{24,28},{29,1},{... | collective-permute-start | bytes 393224 | tf_op jit(solution)/shard_map/while/body/eval_jaxpr/ppermute | solution.py:27
  417.4 10.3 %collective-permute-start.11 = (bf16[128,4,128]{2,0,1:T(8,128)(2,1)S(1)}, bf16[128,4,128]{2,0,1:T(8,128)(2,1)S(1)}, u32[]{:S(2)}, u32[]{:S(2)}) collective-permute-start(bf16[128,4,128]{2,0,1:T(8,128)(2,1)S(1)} %get-tuple-element.3211), channel_id=1, source_target_pairs={{28,0},{0,4},{4,8},{8,12},{12,16},{16,20},{20,24},{24,28},{29,1},{... | collective-permute-start | bytes 393224 | tf_op jit(solution)/shard_map/while/body/eval_jaxpr/ppermute | solution.py:27
  419.7 10.6 %collective-permute-start.12 = (bf16[128,4,128]{2,0,1:T(8,128)(2,1)}, bf16[128,4,128]{2,0,1:T(8,128)(2,1)S(1)}, u32[]{:S(2)}, u32[]{:S(2)}) collective-permute-start(bf16[128,4,128]{2,0,1:T(8,128)(2,1)} %get-tuple-element.3212), channel_id=1, source_target_pairs={{28,0},{0,4},{4,8},{8,12},{12,16},{16,20},{20,24},{24,28},{29,1},{... | collective-permute-start | bytes 393224 | tf_op jit(solution)/shard_map/while/body/eval_jaxpr/ppermute | solution.py:27
  419.9 11.8 %collective-permute-start.13 = (bf16[128,4,128]{2,0,1:T(8,128)(2,1)}, bf16[128,4,128]{2,0,1:T(8,128)(2,1)S(1)}, u32[]{:S(2)}, u32[]{:S(2)}) collective-permute-start(bf16[128,4,128]{2,0,1:T(8,128)(2,1)} %get-tuple-element.3213), channel_id=1, source_target_pairs={{28,0},{0,4},{4,8},{8,12},{12,16},{16,20},{20,24},{24,28},{29,1},{... | collective-permute-start | bytes 393224 | tf_op jit(solution)/shard_map/while/body/eval_jaxpr/ppermute | solution.py:27
  432.5 7.8 %collective-permute-start.10 = (bf16[128,4,128]{2,0,1:T(8,128)(2,1)}, bf16[128,4,128]{2,0,1:T(8,128)(2,1)S(1)}, u32[]{:S(2)}, u32[]{:S(2)}) collective-permute-start(bf16[128,4,128]{2,0,1:T(8,128)(2,1)} %get-tuple-element.3210), channel_id=1, source_target_pairs={{28,0},{0,4},{4,8},{8,12},{12,16},{16,20},{20,24},{24,28},{29,1},{... | collective-permute-start | bytes 393224 | tf_op jit(solution)/shard_map/while/body/eval_jaxpr/ppermute | solution.py:27
  432.5 10.6 %collective-permute-start.11 = (bf16[128,4,128]{2,0,1:T(8,128)(2,1)S(1)}, bf16[128,4,128]{2,0,1:T(8,128)(2,1)S(1)}, u32[]{:S(2)}, u32[]{:S(2)}) collective-permute-start(bf16[128,4,128]{2,0,1:T(8,128)(2,1)S(1)} %get-tuple-element.3211), channel_id=1, source_target_pairs={{28,0},{0,4},{4,8},{8,12},{12,16},{16,20},{20,24},{24,28},{29,1},{... | collective-permute-start | bytes 393224 | tf_op jit(solution)/shard_map/while/body/eval_jaxpr/ppermute | solution.py:27
  434.1 11.9 %collective-permute-start.12 = (bf16[128,4,128]{2,0,1:T(8,128)(2,1)}, bf16[128,4,128]{2,0,1:T(8,128)(2,1)S(1)}, u32[]{:S(2)}, u32[]{:S(2)}) collective-permute-start(bf16[128,4,128]{2,0,1:T(8,128)(2,1)} %get-tuple-element.3212), channel_id=1, source_target_pairs={{28,0},{0,4},{4,8},{8,12},{12,16},{16,20},{20,24},{24,28},{29,1},{... | collective-permute-start | bytes 393224 | tf_op jit(solution)/shard_map/while/body/eval_jaxpr/ppermute | solution.py:27
  434.9 13.3 %collective-permute-start.13 = (bf16[128,4,128]{2,0,1:T(8,128)(2,1)}, bf16[128,4,128]{2,0,1:T(8,128)(2,1)S(1)}, u32[]{:S(2)}, u32[]{:S(2)}) collective-permute-start(bf16[128,4,128]{2,0,1:T(8,128)(2,1)} %get-tuple-element.3213), channel_id=1, source_target_pairs={{28,0},{0,4},{4,8},{8,12},{12,16},{16,20},{20,24},{24,28},{29,1},{... | collective-permute-start | bytes 393224 | tf_op jit(solution)/shard_map/while/body/eval_jaxpr/ppermute | solution.py:27
  449.1 8.8 %collective-permute-start.10 = (bf16[128,4,128]{2,0,1:T(8,128)(2,1)}, bf16[128,4,128]{2,0,1:T(8,128)(2,1)S(1)}, u32[]{:S(2)}, u32[]{:S(2)}) collective-permute-start(bf16[128,4,128]{2,0,1:T(8,128)(2,1)} %get-tuple-element.3210), channel_id=1, source_target_pairs={{28,0},{0,4},{4,8},{8,12},{12,16},{16,20},{20,24},{24,28},{29,1},{... | collective-permute-start | bytes 393224 | tf_op jit(solution)/shard_map/while/body/eval_jaxpr/ppermute | solution.py:27
  449.1 11.6 %collective-permute-start.11 = (bf16[128,4,128]{2,0,1:T(8,128)(2,1)S(1)}, bf16[128,4,128]{2,0,1:T(8,128)(2,1)S(1)}, u32[]{:S(2)}, u32[]{:S(2)}) collective-permute-start(bf16[128,4,128]{2,0,1:T(8,128)(2,1)S(1)} %get-tuple-element.3211), channel_id=1, source_target_pairs={{28,0},{0,4},{4,8},{8,12},{12,16},{16,20},{20,24},{24,28},{29,1},{... | collective-permute-start | bytes 393224 | tf_op jit(solution)/shard_map/while/body/eval_jaxpr/ppermute | solution.py:27
  450.8 12.7 %collective-permute-start.12 = (bf16[128,4,128]{2,0,1:T(8,128)(2,1)}, bf16[128,4,128]{2,0,1:T(8,128)(2,1)S(1)}, u32[]{:S(2)}, u32[]{:S(2)}) collective-permute-start(bf16[128,4,128]{2,0,1:T(8,128)(2,1)} %get-tuple-element.3212), channel_id=1, source_target_pairs={{28,0},{0,4},{4,8},{8,12},{12,16},{16,20},{20,24},{24,28},{29,1},{... | collective-permute-start | bytes 393224 | tf_op jit(solution)/shard_map/while/body/eval_jaxpr/ppermute | solution.py:27
  452.4 12.6 %collective-permute-start.13 = (bf16[128,4,128]{2,0,1:T(8,128)(2,1)}, bf16[128,4,128]{2,0,1:T(8,128)(2,1)S(1)}, u32[]{:S(2)}, u32[]{:S(2)}) collective-permute-start(bf16[128,4,128]{2,0,1:T(8,128)(2,1)} %get-tuple-element.3213), channel_id=1, source_target_pairs={{28,0},{0,4},{4,8},{8,12},{12,16},{16,20},{20,24},{24,28},{29,1},{... | collective-permute-start | bytes 393224 | tf_op jit(solution)/shard_map/while/body/eval_jaxpr/ppermute | solution.py:27
  465.8 9.1 %collective-permute-start.11 = (bf16[128,4,128]{2,0,1:T(8,128)(2,1)S(1)}, bf16[128,4,128]{2,0,1:T(8,128)(2,1)S(1)}, u32[]{:S(2)}, u32[]{:S(2)}) collective-permute-start(bf16[128,4,128]{2,0,1:T(8,128)(2,1)S(1)} %get-tuple-element.3211), channel_id=1, source_target_pairs={{28,0},{0,4},{4,8},{8,12},{12,16},{16,20},{20,24},{24,28},{29,1},{... | collective-permute-start | bytes 393224 | tf_op jit(solution)/shard_map/while/body/eval_jaxpr/ppermute | solution.py:27
  468.3 8.1 %collective-permute-start.12 = (bf16[128,4,128]{2,0,1:T(8,128)(2,1)}, bf16[128,4,128]{2,0,1:T(8,128)(2,1)S(1)}, u32[]{:S(2)}, u32[]{:S(2)}) collective-permute-start(bf16[128,4,128]{2,0,1:T(8,128)(2,1)} %get-tuple-element.3212), channel_id=1, source_target_pairs={{28,0},{0,4},{4,8},{8,12},{12,16},{16,20},{20,24},{24,28},{29,1},{... | collective-permute-start | bytes 393224 | tf_op jit(solution)/shard_map/while/body/eval_jaxpr/ppermute | solution.py:27
  469.7 8.1 %collective-permute-start.13 = (bf16[128,4,128]{2,0,1:T(8,128)(2,1)}, bf16[128,4,128]{2,0,1:T(8,128)(2,1)S(1)}, u32[]{:S(2)}, u32[]{:S(2)}) collective-permute-start(bf16[128,4,128]{2,0,1:T(8,128)(2,1)} %get-tuple-element.3213), channel_id=1, source_target_pairs={{28,0},{0,4},{4,8},{8,12},{12,16},{16,20},{20,24},{24,28},{29,1},{... | collective-permute-start | bytes 393224 | tf_op jit(solution)/shard_map/while/body/eval_jaxpr/ppermute | solution.py:27
  478.7 11.9 %collective-permute-start.10 = (bf16[128,4,128]{2,0,1:T(8,128)(2,1)}, bf16[128,4,128]{2,0,1:T(8,128)(2,1)S(1)}, u32[]{:S(2)}, u32[]{:S(2)}) collective-permute-start(bf16[128,4,128]{2,0,1:T(8,128)(2,1)} %get-tuple-element.3210), channel_id=1, source_target_pairs={{28,0},{0,4},{4,8},{8,12},{12,16},{16,20},{20,24},{24,28},{29,1},{... | collective-permute-start | bytes 393224 | tf_op jit(solution)/shard_map/while/body/eval_jaxpr/ppermute | solution.py:27
  479.8 11.4 %collective-permute-start.11 = (bf16[128,4,128]{2,0,1:T(8,128)(2,1)S(1)}, bf16[128,4,128]{2,0,1:T(8,128)(2,1)S(1)}, u32[]{:S(2)}, u32[]{:S(2)}) collective-permute-start(bf16[128,4,128]{2,0,1:T(8,128)(2,1)S(1)} %get-tuple-element.3211), channel_id=1, source_target_pairs={{28,0},{0,4},{4,8},{8,12},{12,16},{16,20},{20,24},{24,28},{29,1},{... | collective-permute-start | bytes 393224 | tf_op jit(solution)/shard_map/while/body/eval_jaxpr/ppermute | solution.py:27
  484.9 7.8 %collective-permute-start.12 = (bf16[128,4,128]{2,0,1:T(8,128)(2,1)}, bf16[128,4,128]{2,0,1:T(8,128)(2,1)S(1)}, u32[]{:S(2)}, u32[]{:S(2)}) collective-permute-start(bf16[128,4,128]{2,0,1:T(8,128)(2,1)} %get-tuple-element.3212), channel_id=1, source_target_pairs={{28,0},{0,4},{4,8},{8,12},{12,16},{16,20},{20,24},{24,28},{29,1},{... | collective-permute-start | bytes 393224 | tf_op jit(solution)/shard_map/while/body/eval_jaxpr/ppermute | solution.py:27
  495.4 8.7 %collective-permute-start.14 = (bf16[64,4,128]{2,0,1:T(8,128)(2,1)S(1)}, bf16[64,4,128]{2,0,1:T(8,128)(2,1)S(1)}, u32[]{:S(2)}, u32[]{:S(2)}) collective-permute-start(bf16[64,4,128]{2,0,1:T(8,128)(2,1)S(1)} %get-tuple-element.3102), channel_id=1, source_target_pairs={{28,0},{0,4},{4,8},{8,12},{12,16},{16,20},{20,24},{24,28},{29,1},{... | collective-permute-start | bytes 196616 | tf_op jit(solution)/shard_map/while/body/eval_jaxpr/ppermute | solution.py:27
  496.6 7.7 %collective-permute-start.15 = (bf16[64,4,128]{2,0,1:T(8,128)(2,1)S(1)}, bf16[64,4,128]{2,0,1:T(8,128)(2,1)S(1)}, u32[]{:S(2)}, u32[]{:S(2)}) collective-permute-start(bf16[64,4,128]{2,0,1:T(8,128)(2,1)S(1)} %get-tuple-element.3103), channel_id=1, source_target_pairs={{28,0},{0,4},{4,8},{8,12},{12,16},{16,20},{20,24},{24,28},{29,1},{... | collective-permute-start | bytes 196616 | tf_op jit(solution)/shard_map/while/body/eval_jaxpr/ppermute | solution.py:27
  506.2 10.0 %collective-permute-start.14 = (bf16[64,4,128]{2,0,1:T(8,128)(2,1)S(1)}, bf16[64,4,128]{2,0,1:T(8,128)(2,1)S(1)}, u32[]{:S(2)}, u32[]{:S(2)}) collective-permute-start(bf16[64,4,128]{2,0,1:T(8,128)(2,1)S(1)} %get-tuple-element.3102), channel_id=1, source_target_pairs={{28,0},{0,4},{4,8},{8,12},{12,16},{16,20},{20,24},{24,28},{29,1},{... | collective-permute-start | bytes 196616 | tf_op jit(solution)/shard_map/while/body/eval_jaxpr/ppermute | solution.py:27
  508.6 7.8 %collective-permute-start.15 = (bf16[64,4,128]{2,0,1:T(8,128)(2,1)S(1)}, bf16[64,4,128]{2,0,1:T(8,128)(2,1)S(1)}, u32[]{:S(2)}, u32[]{:S(2)}) collective-permute-start(bf16[64,4,128]{2,0,1:T(8,128)(2,1)S(1)} %get-tuple-element.3103), channel_id=1, source_target_pairs={{28,0},{0,4},{4,8},{8,12},{12,16},{16,20},{20,24},{24,28},{29,1},{... | collective-permute-start | bytes 196616 | tf_op jit(solution)/shard_map/while/body/eval_jaxpr/ppermute | solution.py:27
  541.0 8.0 %collective-permute-start.14 = (bf16[64,4,128]{2,0,1:T(8,128)(2,1)S(1)}, bf16[64,4,128]{2,0,1:T(8,128)(2,1)S(1)}, u32[]{:S(2)}, u32[]{:S(2)}) collective-permute-start(bf16[64,4,128]{2,0,1:T(8,128)(2,1)S(1)} %get-tuple-element.3102), channel_id=1, source_target_pairs={{28,0},{0,4},{4,8},{8,12},{12,16},{16,20},{20,24},{24,28},{29,1},{... | collective-permute-start | bytes 196616 | tf_op jit(solution)/shard_map/while/body/eval_jaxpr/ppermute | solution.py:27
  572.3 15.6 %collective-permute-start.21 = (bf16[256,4,128]{0,2,1:T(8,128)(2,1)S(1)}, bf16[256,4,128]{0,2,1:T(8,128)(2,1)}, u32[]{:S(2)}, u32[]{:S(2)}) collective-permute-start(bf16[256,4,128]{0,2,1:T(8,128)(2,1)S(1)} %copy.534), channel_id=1, source_target_pairs={{12,0},{16,4},{20,8},{24,12},{28,16},{0,20},{4,24},{8,28},{13,1},{... | collective-permute-start | bytes 786440 | tf_op jit(solution)/shard_map/ppermute | solution.py:27
  575.9 11.8 %collective-permute-start.22 = (bf16[128,4,128]{2,0,1:T(8,128)(2,1)S(1)}, bf16[128,4,128]{2,0,1:T(8,128)(2,1)S(1)}, u32[]{:S(2)}, u32[]{:S(2)}) collective-permute-start(bf16[128,4,128]{2,0,1:T(8,128)(2,1)S(1)} %copy-done.37), channel_id=1, source_target_pairs={{28,0},{0,4},{4,8},{8,12},{12,16},{16,20},{20,24},{24,28},{29,1},{... | collective-permute-start | bytes 393224 | tf_op jit(solution)/shard_map/ppermute | solution.py:27
  576.0 11.9 %collective-permute-start.19 = (bf16[128,4,128]{2,0,1:T(8,128)(2,1)S(1)}, bf16[128,4,128]{2,0,1:T(8,128)(2,1)S(1)}, u32[]{:S(2)}, u32[]{:S(2)}) collective-permute-start(bf16[128,4,128]{2,0,1:T(8,128)(2,1)S(1)} %copy-done.36), channel_id=1, source_target_pairs={{28,0},{0,4},{4,8},{8,12},{12,16},{16,20},{20,24},{24,28},{29,1},{... | collective-permute-start | bytes 393224 | tf_op jit(solution)/shard_map/ppermute | solution.py:27
  (133 other events, 3563.7 us)
Sparse Core Ops, SparseCore 0:
  9.6 23.7 all-gather.1
where the time goes:
time: 607 us; the launch traced here: 601 us
  waiting for transfers between devices  212 us (35%)
  starting transfers between devices  164 us (27%)
  matrix products  97.1 us (16%)
  local copies, waits for them, and re-layouts  60.5 us (10%)
  other arithmetic  49.6 us (8%)
  between operations  15.6 us (3%)
    ppermute x108, waiting for transfers between devices, passed_along(): return lax.ppermute(block, axis, route)  199 us
    ppermute x108, starting transfers between devices, passed_along(): return lax.ppermute(block, axis, route)  164 us
    select_n x37, other arithmetic, linked_pairs(): return (query_pos // segment == key_pos // segment) & (key_pos <= query_pos)  19.6 us
    dot_general x18, matrix products, tile_grads(): jnp.einsum('ahd,bhd->hab', query_pack, key_pair[0], preferred_element_typ...  15.2 us
    dot_general x20, matrix products, forward_tile(): jnp.einsum('hab,bhd->ahd', weights_high, key_pair[1], preferred_element_t...  14.8 us
    dot_general x20, matrix products, forward_tile(): jnp.einsum('hab,bhd->ahd', weights_rest, key_pair[1], preferred_element_t...  14.4 us
    broadcast_in_dim x28, local copies, waits for them, and re-layouts, spread_rows(): jnp.where(chosen, packed[:, None], jnp.asarray(fill_value, packed.dtype))  12.8 us
    all_gather x1, waiting for transfers between devices, local(): lax.all_gather(out_grad, 'tp', axis=1, tiled=True)  12.5 us
  transfers between devices with their start and end apart: 109, of which 85 were waited for; matrix products, arithmetic and copies ran while one was open for 17% of the time, Pallas kernels for 0%

commit v1 on v0

v1 whole, which is shorter than its diff:
```python
import functools
import math

import jax
import jax.numpy as jnp
from jax import lax
from jax.experimental import pallas as pl
from jax.experimental.pallas import tpu as pltpu
from jax.sharding import PartitionSpec as P

LEVELS = 3
KEYS_SEG = 1024
MESH = pl.DeviceIdType.MESH
NEGATIVE_FILL = -1e30
CHUNKS = 4
SUB = 128
F32 = jnp.float32
BF16 = jnp.bfloat16


def nt(a, b):
    return lax.dot_general(a, b, (((1,), (1,)), ((), ())), preferred_element_type=F32)


def tn(a, b):
    return lax.dot_general(a, b, (((0,), (0,)), ((), ())), preferred_element_type=F32)


def kernel(
    n, q_ref, k_ref, v_ref, og_ref, w_hbm, off_ref, dq_ref, dk_ref, dv_ref,
    w_buf, og_buf, grad_buf, q_buf, g_buf, kv_buf, s_buf, p_buf, ds_buf, wl_buf,
    dkv_acc, dkv_low, dq_low, part_buf,
    w_sem, og_send, og_recv, fw_send, fw_recv, pair_send, pair_recv,
    kv_send, kv_recv, q_send, q_recv, g_send, g_recv,
    dq_send, dq_recv, part_send, part_recv,
):
    tok, width = q_ref.shape
    heads = off_ref.shape[0]
    dim = width // heads
    feats = og_ref.shape[1]
    group = min(KEYS_SEG * 2 ** (LEVELS - 1), tok * n) // tok
    pairs = group // 2
    rows = 2 * tok
    quads = n // 4
    turns = group // 4
    wide = n > group
    me = lax.axis_index("ctx")
    tp = lax.axis_index("tp")
    quad, head = me // 4, me % 4
    start = (4 * quad) % group
    straddle = start == 0
    u_block = (me + n - 2) % n
    own_group, own_slot = u_block // group, u_block % group
    first_group = ((4 * quad + n - 2) % n) // group
    core_peer = tp + 1 - 2 * (tp % 2)
    y_peer = (tp + 2) % 4
    far_peer = (core_peer + 2) % 4

    def move(src, dst, send, recv, target):
        @pl.when(target != me)
        def _():
            pltpu.make_async_remote_copy(
                src_ref=src, dst_ref=dst, send_sem=send, recv_sem=recv,
                device_id={"ctx": target}, device_id_type=MESH,
            ).start()

        @pl.when(target == me)
        def _():
            pltpu.make_async_copy(src, dst, recv).start()

    def sent(src, send, target):
        @pl.when(target != me)
        def _():
            pltpu.make_async_copy(src, src, send).wait()

    def arrived(dst, recv):
        pltpu.make_async_copy(dst, dst, recv).wait()

    def cols(index):
        return pl.ds(pl.multiple_of(index * dim, dim), dim)

    def block(index, size):
        return pl.ds(pl.multiple_of(index * size, size), size)

    w_copy = pltpu.make_async_copy(w_hbm, w_buf, w_sem)
    w_copy.start()

    barrier = pltpu.get_barrier_semaphore()
    for step in range(1, n):
        pl.semaphore_signal(
            barrier, inc=1, device_id={"ctx": (me + step) % n}, device_id_type=MESH
        )
    for peer in (core_peer, y_peer):
        pl.semaphore_signal(barrier, inc=1, device_id={"tp": peer}, device_id_type=MESH)
    pl.semaphore_wait(barrier, n + 1)

    def tp_copy(src, dst, send, recv, peer):
        return pltpu.make_async_remote_copy(
            src_ref=src, dst_ref=dst, send_sem=send, recv_sem=recv,
            device_id={"tp": peer}, device_id_type=MESH,
        )

    piece = feats // CHUNKS
    for c in range(CHUNKS):
        part = pl.ds(c * piece, piece)
        tp_copy(
            og_ref.at[:, part], og_buf.at[1, :, part], og_send.at[c], og_recv.at[c], y_peer
        ).start()
    tp_copy(og_ref, og_buf.at[0], pair_send, pair_recv, core_peer).start()

    sources = (k_ref, v_ref)

    def turn_list():
        listed = []
        for j in range(1, turns + 1):
            needed = own_slot <= 4 * j + 1
            listed.append((j, j - 1, needed, own_slot))
        if wide:
            listed.append((0, turns, own_slot < 2, group + own_slot))
        return listed

    def each_kv(act):
        for j, at, needed, slot in turn_list():
            @pl.when(needed)
            def _(j=j, at=at, slot=slot):
                to_quad = (own_group * turns + j) % quads
                for h in range(4):
                    for kind in range(2):
                        act(kind, at, h, slot, 4 * to_quad + h)

    for h in range(4):
        move(
            q_ref.at[:, pl.ds(h * dim, dim)], q_buf.at[block(head, tok)],
            q_send.at[h], q_recv.at[head], 4 * quad + h,
        )
    each_kv(
        lambda kind, at, h, slot, target: move(
            sources[kind].at[:, pl.ds(h * dim, dim)], kv_buf.at[kind, block(slot, tok)],
            kv_send.at[kind, at, h], kv_recv.at[kind, slot], target,
        )
    )

    dkv_acc[...] = jnp.zeros_like(dkv_acc)

    w_copy.wait()

    def w_part(shard, c):
        return w_buf[:, pl.ds(pl.multiple_of(shard * feats + c * piece, piece), piece)]

    total = nt(og_ref[...], w_buf[:, block(tp, feats)])
    arrived(og_buf.at[0], pair_recv)
    total += nt(og_buf[0], w_buf[:, block(core_peer, feats)])
    for c in range(CHUNKS):
        part = pl.ds(c * piece, piece)
        arrived(og_buf.at[1, :, part], og_recv.at[c])
        tp_copy(
            og_buf.at[1, :, part], og_buf.at[2, :, part], fw_send.at[c], fw_recv.at[c], core_peer
        ).start()
        total += nt(og_buf[1, :, part], w_part(y_peer, c))
    for c in range(CHUNKS):
        part = pl.ds(c * piece, piece)
        arrived(og_buf.at[2, :, part], fw_recv.at[c])
        total += nt(og_buf[2, :, part], w_part(far_peer, c))
    grad_buf[...] = total.astype(BF16)
    for h in range(4):
        move(
            grad_buf.at[:, pl.ds(h * dim, dim)], g_buf.at[block(head, tok)],
            g_send.at[h], g_recv.at[head], 4 * quad + h,
        )

    def slot_needed(slot):
        return straddle | (slot <= start + 1)

    def each_slot(act):
        for slot in range(group):
            pl.when(slot_needed(slot))(functools.partial(act, slot))
        if wide:
            for slot in range(group, group + 2):
                pl.when(straddle)(functools.partial(act, slot))

    def wait_kind(kind):
        each_slot(lambda slot: arrived(kv_buf.at[kind, block(slot, tok)], kv_recv.at[kind, slot]))

    for b in range(4):
        arrived(q_buf.at[block(b, tok)], q_recv.at[b])
    wait_kind(0)

    odd1, odd2 = off_ref[head, 1], off_ref[head, 2]
    key_row = lax.broadcasted_iota(jnp.int32, (8, rows), 0)
    query_col = lax.broadcasted_iota(jnp.int32, (8, rows), 1)
    both1 = ((key_row % 2 == odd1) & (query_col % 2 == odd1)).astype(F32)
    both2 = ((key_row % 4 == odd2) & (query_col % 4 == odd2)).astype(F32)
    sub_row = lax.broadcasted_iota(jnp.int32, (SUB, rows), 0)
    sub_col = lax.broadcasted_iota(jnp.int32, (SUB, rows), 1)
    score_scale = 1.0 / math.sqrt(dim)
    to_exp2 = score_scale / math.log(2.0)
    halves = []
    for half in range(2):
        if half == 0:
            at_pair = jnp.where(straddle, pairs - 1, start // 2 - 1)
            base = 0
        else:
            at_pair = jnp.where(straddle, 0, start // 2)
            base = jnp.where(straddle, pairs, 0) if wide else 0
        halves.append((at_pair, base))

    def folded(values):
        return values.reshape(values.shape[0] // 8, 8, values.shape[1])

    tops = []
    for half, (at_pair, base) in enumerate(halves):
        queries = q_buf[half * rows:(half + 1) * rows, :]

        def score_body(kp, top, half=half, at_pair=at_pair, base=base, queries=queries):
            same0 = jnp.where(at_pair // 2 == kp // 2, 1.0, 0.0)
            same1 = jnp.where(at_pair // 4 == kp // 4, 1.0, 0.0)
            count = same0 + same1 * both1 + both2
            bias = jnp.where(
                count > 2.5, math.log2(3.0),
                jnp.where(count > 1.5, 1.0, jnp.where(count > 0.5, 0.0, NEGATIVE_FILL)),
            )
            lead = (at_pair - kp) * rows
            for s in range(rows // SUB):
                keys = kv_buf[0, pl.ds(pl.multiple_of((base + kp) * rows + s * SUB, SUB), SUB), :]
                scores = folded(nt(keys, queries) * to_exp2) + bias[None]
                scores = scores.reshape(SUB, rows)
                scores = jnp.where(sub_row + s * SUB <= sub_col + lead, scores, NEGATIVE_FILL)
                s_buf[half, kp, s * SUB:(s + 1) * SUB, :] = scores
                top = jnp.maximum(top, jnp.max(folded(scores), axis=0))
            return top

        top = lax.fori_loop(
            0, at_pair + 1, score_body, jnp.full((8, rows), NEGATIVE_FILL, F32)
        )
        tops.append(jnp.max(top, axis=0, keepdims=True))

    wait_kind(1)
    for b in range(4):
        arrived(g_buf.at[block(b, tok)], g_recv.at[b])

    part_at = jnp.where(straddle, turns, start // 4) - 1

    def slot_owner(slot):
        return (first_group * group + slot + 2) % n

    def send_slot(slot, owner, at):
        for kind in range(2):
            move(
                dkv_low.at[kind, block(slot, tok)], part_buf.at[kind, at, :, cols(head)],
                part_send.at[kind, slot], part_recv.at[kind, at, head], owner,
            )

    def round_pair(kp):
        dkv_low[0, block(kp, rows), :] = (dkv_acc[0, block(kp, rows), :] * score_scale).astype(BF16)
        dkv_low[1, block(kp, rows), :] = dkv_acc[1, block(kp, rows), :].astype(BF16)

    def send_pair(kp):
        round_pair(kp)
        for b in range(2):
            slot = 2 * kp + b
            send_slot(slot, slot_owner(slot), part_at)

    shared = jnp.where(straddle, 0, halves[1][0] + 1) if wide else halves[1][0] + 1

    for half, (at_pair, base) in enumerate(halves):
        queries = q_buf[half * rows:(half + 1) * rows, :]
        grads = g_buf[half * rows:(half + 1) * rows, :]
        top = tops[half]

        def weigh_body(kp, sums, half=half, base=base, grads=grads, top=top):
            den, num = sums
            for s in range(rows // SUB):
                here = slice(s * SUB, (s + 1) * SUB)
                vals = kv_buf[1, pl.ds(pl.multiple_of((base + kp) * rows + s * SUB, SUB), SUB), :]
                prob = nt(vals, grads)
                weight = jnp.exp2(s_buf[half, kp, here, :] - top)
                s_buf[half, kp, here, :] = weight
                p_buf[kp, here, :] = prob
                den = den + jnp.sum(folded(weight), axis=0)
                num = num + jnp.sum(folded(weight * prob), axis=0)
            return den, num

        zero = jnp.zeros((8, rows), F32)
        den, num = lax.fori_loop(0, at_pair + 1, weigh_body, (zero, zero))
        inverse = 1.0 / jnp.sum(den, axis=0, keepdims=True)
        delta = jnp.sum(num, axis=0, keepdims=True) * inverse

        def grad_body(
            kp, total, half=half, base=base, queries=queries, grads=grads,
            inverse=inverse, delta=delta,
        ):
            for s in range(rows // SUB):
                here = slice(s * SUB, (s + 1) * SUB)
                weight = s_buf[half, kp, here, :] * inverse
                wl_buf[here, :] = weight.astype(BF16)
                ds_buf[here, :] = (weight * (p_buf[kp, here, :] - delta)).astype(BF16)
            place = block(base + kp, rows)
            score_grad = ds_buf[...]
            dkv_acc[0, place, :] += jnp.dot(score_grad, queries, preferred_element_type=F32)
            dkv_acc[1, place, :] += jnp.dot(wl_buf[...], grads, preferred_element_type=F32)
            total = total + tn(kv_buf[0, place, :], score_grad)
            if half == 1:
                if wide:
                    pl.when(jnp.logical_not(straddle))(functools.partial(send_pair, kp))
                else:
                    send_pair(kp)
            return total

        total = lax.fori_loop(0, at_pair + 1, grad_body, jnp.zeros((dim, rows), F32))
        dq_low[half * rows:(half + 1) * rows, :] = (total * score_scale).T.astype(BF16)
        for b in range(2 * half, 2 * half + 2):
            move(
                dq_low.at[pl.ds(b * tok, tok)], dq_ref.at[:, cols(head)],
                dq_send.at[b], dq_recv.at[head], 4 * quad + b,
            )
        if half == 0:
            lax.fori_loop(shared, at_pair + 1, lambda kp, none: (send_pair(kp), none)[1], 0)
    if wide:
        @pl.when(straddle)
        def _():
            round_pair(pairs)
            for b in range(2):
                send_slot(group + b, (4 * quad + b + 2) % n, turns)

    for j, at, needed, slot in turn_list():
        @pl.when(needed)
        def _(at=at):
            for kind in range(2):
                for h in range(4):
                    arrived(part_buf.at[kind, at, :, pl.ds(h * dim, dim)], part_recv.at[kind, at, h])
    for kind, out in ((0, dk_ref), (1, dv_ref)):
        dkv_sum = part_buf[kind, turns - 1].astype(F32)
        for j, at, needed, slot in turn_list():
            if at != turns - 1:
                dkv_sum = dkv_sum + jnp.where(needed, part_buf[kind, at].astype(F32), 0.0)
        out[...] = dkv_sum.astype(BF16)
    for h in range(4):
        arrived(dq_ref.at[:, pl.ds(h * dim, dim)], dq_recv.at[h])

    for c in range(CHUNKS):
        part = pl.ds(c * piece, piece)
        pltpu.make_async_copy(og_ref.at[:, part], og_ref.at[:, part], og_send.at[c]).wait()
        pltpu.make_async_copy(og_ref.at[:, part], og_ref.at[:, part], fw_send.at[c]).wait()
    pltpu.make_async_copy(og_ref, og_ref, pair_send).wait()
    for h in range(4):
        sent(q_ref.at[:, pl.ds(h * dim, dim)], q_send.at[h], 4 * quad + h)
        sent(grad_buf.at[:, pl.ds(h * dim, dim)], g_send.at[h], 4 * quad + h)
        sent(dq_low.at[pl.ds(h * tok, tok)], dq_send.at[h], 4 * quad + h)
    each_kv(
        lambda kind, at, h, slot, target: sent(
            sources[kind].at[:, pl.ds(h * dim, dim)], kv_send.at[kind, at, h], target
        )
    )

    def slot_sent(slot):
        owner = slot_owner(slot) if slot < group else (4 * quad + slot - group + 2) % n
        for kind in range(2):
            sent(dkv_low.at[kind, pl.ds(slot * tok, tok)], part_send.at[kind, slot], owner)

    each_slot(slot_sent)


def local(queries, keys, values, out_grad, w_out, offsets):
    n = lax.axis_size("ctx")
    tok, width = queries.shape
    heads = offsets.shape[0]
    dim = width // heads
    feats = out_grad.shape[1]
    group = min(KEYS_SEG * 2 ** (LEVELS - 1), tok * n) // tok
    assert heads == 4 and tok * 4 == KEYS_SEG and lax.axis_size("tp") == 4
    assert n % group == 0 and group % 4 == 0
    pairs, rows, turns = group // 2, 2 * tok, group // 4
    wide = n > group
    slots = group + 2 * wide
    kinds = turns + wide
    dma = pltpu.SemaphoreType.DMA
    vmem = pl.BlockSpec(memory_space=pltpu.VMEM)
    out = jax.ShapeDtypeStruct((tok, width), BF16)
    return pl.pallas_call(
        functools.partial(kernel, n),
        out_shape=(out, out, out),
        in_specs=[vmem, vmem, vmem, vmem, pl.BlockSpec(memory_space=pl.ANY),
                  pl.BlockSpec(memory_space=pltpu.SMEM)],
        out_specs=(vmem, vmem, vmem),
        scratch_shapes=[
            pltpu.VMEM(w_out.shape, BF16),
            pltpu.VMEM((3, tok, feats), BF16),
            pltpu.VMEM((tok, width), BF16),
            pltpu.VMEM((4 * tok, dim), BF16),
            pltpu.VMEM((4 * tok, dim), BF16),
            pltpu.VMEM((2, slots * tok, dim), BF16),
            pltpu.VMEM((2, pairs, rows, rows), F32),
            pltpu.VMEM((pairs, rows, rows), F32),
            pltpu.VMEM((rows, rows), BF16),
            pltpu.VMEM((rows, rows), BF16),
            pltpu.VMEM((2, slots * tok, dim), F32),
            pltpu.VMEM((2, slots * tok, dim), BF16),
            pltpu.VMEM((4 * tok, dim), BF16),
            pltpu.VMEM((2, kinds, tok, width), BF16),
            dma, dma((CHUNKS,)), dma((CHUNKS,)), dma((CHUNKS,)), dma((CHUNKS,)), dma, dma,
            dma((2, kinds, 4)), dma((2, slots)), dma((4,)), dma((4,)), dma((4,)), dma((4,)),
            dma((4,)), dma((4,)), dma((2, slots)), dma((2, kinds, 4)),
        ],
        compiler_params=pltpu.CompilerParams(
            collective_id=0, has_side_effects=True, vmem_limit_bytes=56 * 1024 * 1024
        ),
        cost_estimate=pl.CostEstimate(
            flops=5 * 10 * rows * rows * dim + 2 * tok * width * feats * 4,
            bytes_accessed=2 * (w_out.size + 8 * tok * width), transcendentals=5 * rows * rows,
        ),
    )(queries, keys, values, out_grad, w_out, offsets)


def solution(mesh):
    return jax.shard_map(
        local,
        mesh=mesh,
        in_specs=(
            P("ctx", "tp"),
            P("ctx", "tp"),
            P("ctx", "tp"),
            P("ctx", "tp"),
            P("tp", None),
            P("tp", None),
        ),
        out_specs=(P("ctx", "tp"), P("ctx", "tp"), P("ctx", "tp")),
        check_vma=False,
    )
```

time: 607 us -> 64.4 us (0.11)
  the two profiles are of different devices: /device:TPU:8 before, /device:TPU:27 now
where the time goes in v1:
time: 64.4 us; the launch traced here: 64.1 us
  Pallas kernels  58.5 us (91%)
  local copies, waits for them, and re-layouts  5.01 us (8%)
    pallas_call x1, Pallas kernels, local(): pl.pallas_call(functools.partial(kernel, n), out_shape=(out, out, out), i...  58.5 us
    unnamed x3, local copies, waits for them, and re-layouts  5.01 us

profile of v1, /device:TPU:27, one launch (start us, length us, event | category | flops | bytes accessed | tf_op | source)
XLA Modules:
  0.0 64.1 jit_solution(1265583280252894673)
XLA Ops:
  0.6 58.5 %shard_map.85 = (bf16[256,512]{1,0:T(8,128)(2,1)}, bf16[256,512]{1,0:T(8,128)(2,1)}, bf16[256,512]{1,0:T(8,128)(2,1)}) custom-call(bf16[256,512]{1,0:T(8,128)(2,1)} %q_ref.1, bf16[256,512]{1,0:T(8,128)(2,1)} %k_ref.1, bf16[256,512]{1,0:T(8,128)(2,1)} %v_ref.1, bf16[256,1024]{1,0:T(8,128)(2,1)} %og_ref.1, bf16[512,4096]{1,0:T(8,128)(2,1)} %w_hbm.1, ...), custom_call_target="tpu_custom_call" | custom-call | flops 2751463424 | bytes 6291456 | tf_op jit(solution)/shard_map/pallas_call | solution.py:379
  59.1 1.7 %copy.12 = bf16[256,512]{1,0:T(8,128)(2,1)} copy(bf16[256,512]{1,0:T(8,128)(2,1)} %get-tuple-element.6) | data formatting | bytes 524288
  60.8 1.7 %copy.13 = bf16[256,512]{1,0:T(8,128)(2,1)} copy(bf16[256,512]{1,0:T(8,128)(2,1)} %get-tuple-element.7) | data formatting | bytes 524288
  62.5 1.7 %copy.14 = bf16[256,512]{1,0:T(8,128)(2,1)} copy(bf16[256,512]{1,0:T(8,128)(2,1)} %get-tuple-element.8) | data formatting | bytes 524288

commit v2 on v1

--- a/solution.py
+++ b/solution.py
@@ -26,11 +26,21 @@
     return lax.dot_general(a, b, (((0,), (0,)), ((), ())), preferred_element_type=F32)
 
 
+def owner_turns(group, wide, own_slot):
+    turns = group // 4
+    listed = [(turns, turns - 1, own_slot < group, own_slot)]
+    for j in range(1, turns):
+        listed.append((j, j - 1, own_slot <= 4 * j + 1, own_slot))
+    if wide:
+        listed.append((0, turns, own_slot < 2, group + own_slot))
+    return listed
+
+
 def kernel(
-    n, q_ref, k_ref, v_ref, og_ref, w_hbm, off_ref, dq_ref, dk_ref, dv_ref,
+    n, q_ref, k_ref, v_ref, og_ref, w_hbm, off_ref, dq_ref, part_buf,
     w_buf, og_buf, grad_buf, q_buf, g_buf, kv_buf, s_buf, p_buf, ds_buf, wl_buf,
-    dkv_acc, dkv_low, dq_low, part_buf,
-    w_sem, og_send, og_recv, fw_send, fw_recv, pair_send, pair_recv,
+    dkv_acc, dkv_low, dq_low,
+    w_sem, og_sem, og_send, og_recv, fw_send, fw_recv, pair_send, pair_recv,
     kv_send, kv_recv, q_send, q_recv, g_send, g_recv,
     dq_send, dq_recv, part_send, part_recv,
 ):
@@ -84,6 +94,8 @@
 
     w_copy = pltpu.make_async_copy(w_hbm, w_buf, w_sem)
     w_copy.start()
+    og_copy = pltpu.make_async_copy(og_ref, og_buf.at[3], og_sem)
+    og_copy.start()
 
     barrier = pltpu.get_barrier_semaphore()
     for step in range(1, n):
@@ -109,45 +121,43 @@
     tp_copy(og_ref, og_buf.at[0], pair_send, pair_recv, core_peer).start()
 
     sources = (k_ref, v_ref)
-
-    def turn_list():
-        listed = []
-        for j in range(1, turns + 1):
-            needed = own_slot <= 4 * j + 1
-            listed.append((j, j - 1, needed, own_slot))
-        if wide:
-            listed.append((0, turns, own_slot < 2, group + own_slot))
-        return listed
-
-    def each_kv(act):
-        for j, at, needed, slot in turn_list():
-            @pl.when(needed)
-            def _(j=j, at=at, slot=slot):
-                to_quad = (own_group * turns + j) % quads
-                for h in range(4):
-                    for kind in range(2):
-                        act(kind, at, h, slot, 4 * to_quad + h)
-
+    turn_list = owner_turns(group, wide, own_slot)
+
+    def send_kv(act, kind, entry):
+        j, at, needed, slot = entry
+
+        @pl.when(needed)
+        def _():
+            to_quad = (own_group * turns + j) % quads
+            for h in range(4):
+                act(kind, at, h, slot, 4 * to_quad + h)
+
+    def start_kv(kind, at, h, slot, target):
+        move(
+            sources[kind].at[:, pl.ds(h * dim, dim)], kv_buf.at[kind, block(slot, tok)],
+            kv_send.at[kind, at, h], kv_recv.at[kind, slot], target,
+        )
+
+    send_kv(start_kv, 0, turn_list[0])
     for h in range(4):
         move(
             q_ref.at[:, pl.ds(h * dim, dim)], q_buf.at[block(head, tok)],
             q_send.at[h], q_recv.at[head], 4 * quad + h,
         )
-    each_kv(
-        lambda kind, at, h, slot, target: move(
-            sources[kind].at[:, pl.ds(h * dim, dim)], kv_buf.at[kind, block(slot, tok)],
-            kv_send.at[kind, at, h], kv_recv.at[kind, slot], target,
-        )
-    )
+    send_kv(start_kv, 1, turn_list[0])
+    for kind in range(2):
+        for entry in turn_list[1:]:
+            send_kv(start_kv, kind, entry)
 
     dkv_acc[...] = jnp.zeros_like(dkv_acc)
 
     w_copy.wait()
+    og_copy.wait()
 
     def w_part(shard, c):
         return w_buf[:, pl.ds(pl.multiple_of(shard * feats + c * piece, piece), piece)]
 
-    total = nt(og_ref[...], w_buf[:, block(tp, feats)])
+    total = nt(og_buf[3], w_buf[:, block(tp, feats)])
     arrived(og_buf.at[0], pair_recv)
     total += nt(og_buf[0], w_buf[:, block(core_peer, feats)])
     for c in range(CHUNKS):
@@ -168,22 +178,13 @@
             g_send.at[h], g_recv.at[head], 4 * quad + h,
         )
 
-    def slot_needed(slot):
-        return straddle | (slot <= start + 1)
-
-    def each_slot(act):
-        for slot in range(group):
-            pl.when(slot_needed(slot))(functools.partial(act, slot))
-        if wide:
-            for slot in range(group, group + 2):
-                pl.when(straddle)(functools.partial(act, slot))
-
-    def wait_kind(kind):
-        each_slot(lambda slot: arrived(kv_buf.at[kind, block(slot, tok)], kv_recv.at[kind, slot]))
+    def wait_pair(kind, pair):
+        for b in range(2):
+            slot = 2 * pair + b
+            arrived(kv_buf.at[kind, block(slot, tok)], kv_recv.at[kind, slot])
 
     for b in range(4):
         arrived(q_buf.at[block(b, tok)], q_recv.at[b])
-    wait_kind(0)
 
     odd1, odd2 = off_ref[head, 1], off_ref[head, 2]
     key_row = lax.broadcasted_iota(jnp.int32, (8, rows), 0)
@@ -194,24 +195,35 @@
     sub_col = lax.broadcasted_iota(jnp.int32, (SUB, rows), 1)
     score_scale = 1.0 / math.sqrt(dim)
     to_exp2 = score_scale / math.log(2.0)
-    halves = []
-    for half in range(2):
-        if half == 0:
-            at_pair = jnp.where(straddle, pairs - 1, start // 2 - 1)
-            base = 0
+    first_pair = jnp.where(straddle, 0, start // 2 - 1)
+    first_base = jnp.where(straddle, pairs, 0) if wide else 0
+    last_pair = jnp.where(straddle, pairs - 1, start // 2)
+    early = jnp.where(straddle, 1, 0)
+    halves = [(early, first_pair, first_base), (1 - early, last_pair, 0)]
+
+    def arrival(turn, step):
+        count = halves[turn][1] + 1
+        return step if turn == 0 else (step + jnp.where(straddle, count - 1, 1)) % count
+
+    def wait_new(turn, kind, kp):
+        if turn == 0:
+            wait_pair(kind, first_base + kp)
         else:
-            at_pair = jnp.where(straddle, 0, start // 2)
-            base = jnp.where(straddle, pairs, 0) if wide else 0
-        halves.append((at_pair, base))
+            fresh = kp > first_pair
+            if wide:
+                fresh = fresh | straddle
+            pl.when(fresh)(functools.partial(wait_pair, kind, kp))
 
     def folded(values):
         return values.reshape(values.shape[0] // 8, 8, values.shape[1])
 
     tops = []
-    for half, (at_pair, base) in enumerate(halves):
-        queries = q_buf[half * rows:(half + 1) * rows, :]
-
-        def score_body(kp, top, half=half, at_pair=at_pair, base=base, queries=queries):
+    for turn, (half, at_pair, base) in enumerate(halves):
+        queries = q_buf[block(half, rows), :]
+
+        def score_body(step, top, turn=turn, at_pair=at_pair, base=base, queries=queries):
+            kp = arrival(turn, step)
+            wait_new(turn, 0, kp)
             same0 = jnp.where(at_pair // 2 == kp // 2, 1.0, 0.0)
             same1 = jnp.where(at_pair // 4 == kp // 4, 1.0, 0.0)
             count = same0 + same1 * both1 + both2
@@ -225,7 +237,7 @@
                 scores = folded(nt(keys, queries) * to_exp2) + bias[None]
                 scores = scores.reshape(SUB, rows)
                 scores = jnp.where(sub_row + s * SUB <= sub_col + lead, scores, NEGATIVE_FILL)
-                s_buf[half, kp, s * SUB:(s + 1) * SUB, :] = scores
+                s_buf[turn, kp, s * SUB:(s + 1) * SUB, :] = scores
                 top = jnp.maximum(top, jnp.max(folded(scores), axis=0))
             return top
 
@@ -233,10 +245,6 @@
             0, at_pair + 1, score_body, jnp.full((8, rows), NEGATIVE_FILL, F32)
         )
         tops.append(jnp.max(top, axis=0, keepdims=True))
-
-    wait_kind(1)
-    for b in range(4):
-        arrived(g_buf.at[block(b, tok)], g_recv.at[b])
 
     part_at = jnp.where(straddle, turns, start // 4) - 1
 
@@ -260,21 +268,23 @@
             slot = 2 * kp + b
             send_slot(slot, slot_owner(slot), part_at)
 
-    shared = jnp.where(straddle, 0, halves[1][0] + 1) if wide else halves[1][0] + 1
-
-    for half, (at_pair, base) in enumerate(halves):
-        queries = q_buf[half * rows:(half + 1) * rows, :]
-        grads = g_buf[half * rows:(half + 1) * rows, :]
-        top = tops[half]
-
-        def weigh_body(kp, sums, half=half, base=base, grads=grads, top=top):
+    for turn, (half, at_pair, base) in enumerate(halves):
+        queries = q_buf[block(half, rows), :]
+        for b in range(2):
+            arrived(g_buf.at[block(2 * half + b, tok)], g_recv.at[2 * half + b])
+        grads = g_buf[block(half, rows), :]
+        top = tops[turn]
+
+        def weigh_body(step, sums, turn=turn, base=base, grads=grads, top=top):
+            kp = arrival(turn, step)
+            wait_new(turn, 1, kp)
             den, num = sums
             for s in range(rows // SUB):
                 here = slice(s * SUB, (s + 1) * SUB)
                 vals = kv_buf[1, pl.ds(pl.multiple_of((base + kp) * rows + s * SUB, SUB), SUB), :]
                 prob = nt(vals, grads)
-                weight = jnp.exp2(s_buf[half, kp, here, :] - top)
-                s_buf[half, kp, here, :] = weight
+                weight = jnp.exp2(s_buf[turn, kp, here, :] - top)
+                s_buf[turn, kp, here, :] = weight
                 p_buf[kp, here, :] = prob
                 den = den + jnp.sum(folded(weight), axis=0)
                 num = num + jnp.sum(folded(weight * prob), axis=0)
@@ -286,12 +296,15 @@
         delta = jnp.sum(num, axis=0, keepdims=True) * inverse
 
         def grad_body(
-            kp, total, half=half, base=base, queries=queries, grads=grads,
+            step, total, turn=turn, at_pair=at_pair, base=base, queries=queries, grads=grads,
             inverse=inverse, delta=delta,
         ):
+            kp = step
+            if turn == 1:
+                kp = (step + jnp.where(straddle, 1, 0)) % (at_pair + 1)
             for s in range(rows // SUB):
                 here = slice(s * SUB, (s + 1) * SUB)
-                weight = s_buf[half, kp, here, :] * inverse
+                weight = s_buf[turn, kp, here, :] * inverse
                 wl_buf[here, :] = weight.astype(BF16)
                 ds_buf[here, :] = (weight * (p_buf[kp, here, :] - delta)).astype(BF16)
             place = block(base + kp, rows)
@@ -299,22 +312,17 @@
             dkv_acc[0, place, :] += jnp.dot(score_grad, queries, preferred_element_type=F32)
             dkv_acc[1, place, :] += jnp.dot(wl_buf[...], grads, preferred_element_type=F32)
             total = total + tn(kv_buf[0, place, :], score_grad)
-            if half == 1:
-                if wide:
-                    pl.when(jnp.logical_not(straddle))(functools.partial(send_pair, kp))
-                else:
-                    send_pair(kp)
+            if turn == 1:
+                send_pair(kp)
             return total
 
         total = lax.fori_loop(0, at_pair + 1, grad_body, jnp.zeros((dim, rows), F32))
-        dq_low[half * rows:(half + 1) * rows, :] = (total * score_scale).T.astype(BF16)
-        for b in range(2 * half, 2 * half + 2):
+        dq_low[block(half, rows), :] = (total * score_scale).T.astype(BF16)
+        for b in range(2):
             move(
-                dq_low.at[pl.ds(b * tok, tok)], dq_ref.at[:, cols(head)],
-                dq_send.at[b], dq_recv.at[head], 4 * quad + b,
+                dq_low.at[block(2 * half + b, tok)], dq_ref.at[:, cols(head)],
+                dq_send.at[2 * half + b], dq_recv.at[head], 4 * quad + 2 * half + b,
             )
-        if half == 0:
-            lax.fori_loop(shared, at_pair + 1, lambda kp, none: (send_pair(kp), none)[1], 0)
     if wide:
         @pl.when(straddle)
         def _():
@@ -322,18 +330,12 @@
             for b in range(2):
                 send_slot(group + b, (4 * quad + b + 2) % n, turns)
 
-    for j, at, needed, slot in turn_list():
+    for j, at, needed, slot in turn_list:
         @pl.when(needed)
         def _(at=at):
             for kind in range(2):
                 for h in range(4):
                     arrived(part_buf.at[kind, at, :, pl.ds(h * dim, dim)], part_recv.at[kind, at, h])
-    for kind, out in ((0, dk_ref), (1, dv_ref)):
-        dkv_sum = part_buf[kind, turns - 1].astype(F32)
-        for j, at, needed, slot in turn_list():
-            if at != turns - 1:
-                dkv_sum = dkv_sum + jnp.where(needed, part_buf[kind, at].astype(F32), 0.0)
-        out[...] = dkv_sum.astype(BF16)
     for h in range(4):
         arrived(dq_ref.at[:, pl.ds(h * dim, dim)], dq_recv.at[h])
 
@@ -346,18 +348,33 @@
         sent(q_ref.at[:, pl.ds(h * dim, dim)], q_send.at[h], 4 * quad + h)
         sent(grad_buf.at[:, pl.ds(h * dim, dim)], g_send.at[h], 4 * quad + h)
         sent(dq_low.at[pl.ds(h * tok, tok)], dq_send.at[h], 4 * quad + h)
-    each_kv(
-        lambda kind, at, h, slot, target: sent(
-            sources[kind].at[:, pl.ds(h * dim, dim)], kv_send.at[kind, at, h], target
-        )
-    )
+
+    def kv_sent(kind, at, h, slot, target):
+        sent(sources[kind].at[:, pl.ds(h * dim, dim)], kv_send.at[kind, at, h], target)
+
+    for kind in range(2):
+        for entry in turn_list:
+            send_kv(kv_sent, kind, entry)
 
     def slot_sent(slot):
         owner = slot_owner(slot) if slot < group else (4 * quad + slot - group + 2) % n
         for kind in range(2):
             sent(dkv_low.at[kind, pl.ds(slot * tok, tok)], part_send.at[kind, slot], owner)
 
-    each_slot(slot_sent)
+    for slot in range(group + 2 * wide):
+        needed = straddle | (slot <= start + 1) if slot < group else straddle
+        pl.when(needed)(functools.partial(slot_sent, slot))
+
+
+def add_kernel(n, group, dq_ref, part_ref, dq_out, dk_out, dv_out):
+    own_slot = ((lax.axis_index("ctx") + n - 2) % n) % group
+    dq_out[...] = dq_ref[...]
+    for kind, out in ((0, dk_out), (1, dv_out)):
+        total = None
+        for j, at, needed, slot in owner_turns(group, n > group, own_slot):
+            part = part_ref[kind, at].astype(F32)
+            total = part if total is None else total + jnp.where(needed, part, 0.0)
+        out[...] = total.astype(BF16)
 
 
 def local(queries, keys, values, out_grad, w_out, offsets):
@@ -374,17 +391,16 @@
     slots = group + 2 * wide
     kinds = turns + wide
     dma = pltpu.SemaphoreType.DMA
-    vmem = pl.BlockSpec(memory_space=pltpu.VMEM)
     out = jax.ShapeDtypeStruct((tok, width), BF16)
-    return pl.pallas_call(
+    hbm = pl.BlockSpec(memory_space=pl.ANY)
+    dq_raw, parts = pl.pallas_call(
         functools.partial(kernel, n),
-        out_shape=(out, out, out),
-        in_specs=[vmem, vmem, vmem, vmem, pl.BlockSpec(memory_space=pl.ANY),
-                  pl.BlockSpec(memory_space=pltpu.SMEM)],
-        out_specs=(vmem, vmem, vmem),
+        out_shape=(out, jax.ShapeDtypeStruct((2, kinds, tok, width), BF16)),
+        in_specs=[hbm] * 5 + [pl.BlockSpec(memory_space=pltpu.SMEM)],
+        out_specs=(hbm, hbm),
         scratch_shapes=[
             pltpu.VMEM(w_out.shape, BF16),
-            pltpu.VMEM((3, tok, feats), BF16),
+            pltpu.VMEM((4, tok, feats), BF16),
             pltpu.VMEM((tok, width), BF16),
             pltpu.VMEM((4 * tok, dim), BF16),
             pltpu.VMEM((4 * tok, dim), BF16),
@@ -396,8 +412,7 @@
             pltpu.VMEM((2, slots * tok, dim), F32),
             pltpu.VMEM((2, slots * tok, dim), BF16),
             pltpu.VMEM((4 * tok, dim), BF16),
-            pltpu.VMEM((2, kinds, tok, width), BF16),
-            dma, dma((CHUNKS,)), dma((CHUNKS,)), dma((CHUNKS,)), dma((CHUNKS,)), dma, dma,
+            dma, dma, dma((CHUNKS,)), dma((CHUNKS,)), dma((CHUNKS,)), dma((CHUNKS,)), dma, dma,
             dma((2, kinds, 4)), dma((2, slots)), dma((4,)), dma((4,)), dma((4,)), dma((4,)),
             dma((4,)), dma((4,)), dma((2, slots)), dma((2, kinds, 4)),
         ],
@@ -409,6 +424,16 @@
             bytes_accessed=2 * (w_out.size + 8 * tok * width), transcendentals=5 * rows * rows,
         ),
     )(queries, keys, values, out_grad, w_out, offsets)
+    steps = 2
+    flat = pl.BlockSpec((tok // steps, width), lambda i: (i, 0))
+    return pl.pallas_call(
+        functools.partial(add_kernel, n, group),
+        grid=(steps,),
+        out_shape=(out, out, out),
+        in_specs=[flat, pl.BlockSpec((2, kinds, tok // steps, width), lambda i: (0, 0, i, 0))],
+        out_specs=(flat, flat, flat),
+        compiler_params=pltpu.CompilerParams(vmem_limit_bytes=16 * 1024 * 1024),
+    )(dq_raw, parts)
 
 
 def solution(mesh):

time: 64.4 us -> 58.5 us (0.908)
  the two profiles are of different devices: /device:TPU:27 before, /device:TPU:30 now
where the time goes in v2:
time: 58.5 us; the launch traced here: 58.3 us
  Pallas kernels  55.5 us (95%)
  local copies, waits for them, and re-layouts  2.17 us (4%)
  between operations  0.65 us (1%)
    pallas_call x1, Pallas kernels, local(): pl.pallas_call(functools.partial(kernel, n), out_shape=(out, jax.ShapeDty...  54.5 us
    unnamed x4, local copies, waits for them, and re-layouts  2.17 us

profile of v2, /device:TPU:30, one launch (start us, length us, event | category | flops | bytes accessed | tf_op | source)
XLA Modules:
  0.0 58.3 jit_solution(3092501024435352556)
XLA Ops:
  0.6 54.5 %shard_map.85 = (bf16[256,512]{1,0:T(8,128)(2,1)}, bf16[2,2,256,512]{3,2,1,0:T(8,128)(2,1)}) custom-call(bf16[256,512]{1,0:T(8,128)(2,1)} %q_ref.1, bf16[256,512]{1,0:T(8,128)(2,1)} %k_ref.1, bf16[256,512]{1,0:T(8,128)(2,1)} %v_ref.1, bf16[256,1024]{1,0:T(8,128)(2,1)} %og_ref.1, bf16[512,4096]{1,0:T(8,128)(2,1)} %w_hbm.1, s32[4,3]{1,0:T(4,128)} %off_ref.1), custom_call_target="tpu_custom_call" | custom-call | flops 2751463424 | bytes 6291456 | tf_op jit(solution)/shard_map/pallas_call | solution.py:396
  55.1 0.0 copy-start
  55.2 1.2 %copy-done = bf16[2,2,256,512]{3,2,1,0:T(8,128)(2,1)S(1)} copy-done((bf16[2,2,256,512]{3,2,1,0:T(8,128)(2,1)S(1)}, bf16[2,2,256,512]{3,2,1,0:T(8,128)(2,1)}, u32[]{:S(2)}) %copy-start) | copy-done | bytes 1048600
  56.4 0.0 copy-start.1
  56.4 0.9 %copy-done.1 = bf16[256,512]{1,0:T(8,128)(2,1)S(1)} copy-done((bf16[256,512]{1,0:T(8,128)(2,1)S(1)}, bf16[256,512]{1,0:T(8,128)(2,1)}, u32[]{:S(2)}) %copy-start.1) | copy-done | bytes 262168
  57.3 1.0 %shard_map.86 = (bf16[256,512]{1,0:T(8,128)(2,1)}, bf16[256,512]{1,0:T(8,128)(2,1)}, bf16[256,512]{1,0:T(8,128)(2,1)}) custom-call(bf16[256,512]{1,0:T(8,128)(2,1)S(1)} %copy-done.1, bf16[2,2,256,512]{3,2,1,0:T(8,128)(2,1)S(1)} %copy-done), custom_call_target="tpu_custom_call" | custom-call | tf_op jit(solution)/shard_map/pallas_call | solution.py:429
Async XLA Ops:
  55.1 1.2 %copy-start = (bf16[2,2,256,512]{3,2,1,0:T(8,128)(2,1)S(1)}, bf16[2,2,256,512]{3,2,1,0:T(8,128)(2,1)}, u32[]{:S(2)}) copy-start(bf16[2,2,256,512]{3,2,1,0:T(8,128)(2,1)} %get-tuple-element.6.part_ref) | copy-start | bytes 3145732
  56.4 0.9 %copy-start.1 = (bf16[256,512]{1,0:T(8,128)(2,1)S(1)}, bf16[256,512]{1,0:T(8,128)(2,1)}, u32[]{:S(2)}) copy-start(bf16[256,512]{1,0:T(8,128)(2,1)} %get-tuple-element.5.dq_ref) | copy-start | bytes 786436

commit v3 on v2

--- a/solution.py
+++ b/solution.py
@@ -251,70 +251,94 @@
     def slot_owner(slot):
         return (first_group * group + slot + 2) % n
 
-    def send_slot(slot, owner, at):
-        for kind in range(2):
-            move(
-                dkv_low.at[kind, block(slot, tok)], part_buf.at[kind, at, :, cols(head)],
-                part_send.at[kind, slot], part_recv.at[kind, at, head], owner,
-            )
-
-    def round_pair(kp):
-        dkv_low[0, block(kp, rows), :] = (dkv_acc[0, block(kp, rows), :] * score_scale).astype(BF16)
-        dkv_low[1, block(kp, rows), :] = dkv_acc[1, block(kp, rows), :].astype(BF16)
-
-    def send_pair(kp):
-        round_pair(kp)
+    def send_slot(kind, slot, owner, at):
+        move(
+            dkv_low.at[kind, block(slot, tok)], part_buf.at[kind, at, :, cols(head)],
+            part_send.at[kind, slot], part_recv.at[kind, at, head], owner,
+        )
+
+    def round_pair(kind, kp):
+        done = dkv_acc[kind, block(kp, rows), :]
+        if kind == 0:
+            done = done * score_scale
+        dkv_low[kind, block(kp, rows), :] = done.astype(BF16)
+
+    def send_pair(kind, kp):
+        round_pair(kind, kp)
         for b in range(2):
             slot = 2 * kp + b
-            send_slot(slot, slot_owner(slot), part_at)
-
+            send_slot(kind, slot, slot_owner(slot), part_at)
+
+    def leaving(turn, step):
+        if turn == 0:
+            return step
+        return (step + jnp.where(straddle, 1, 0)) % (halves[1][1] + 1)
+
+    zero = jnp.zeros((8, rows), F32)
+    inverses = []
     for turn, (half, at_pair, base) in enumerate(halves):
-        queries = q_buf[block(half, rows), :]
+        def weigh_body(step, den, turn=turn, top=tops[turn]):
+            for s in range(rows // SUB):
+                here = slice(s * SUB, (s + 1) * SUB)
+                weight = jnp.exp2(s_buf[turn, step, here, :] - top)
+                s_buf[turn, step, here, :] = weight
+                den = den + jnp.sum(folded(weight), axis=0)
+            return den
+
+        den = lax.fori_loop(0, at_pair + 1, weigh_body, zero)
+        inverses.append(1.0 / jnp.sum(den, axis=0, keepdims=True))
+
+    for turn, (half, at_pair, base) in enumerate(halves):
         for b in range(2):
             arrived(g_buf.at[block(2 * half + b, tok)], g_recv.at[2 * half + b])
         grads = g_buf[block(half, rows), :]
-        top = tops[turn]
-
-        def weigh_body(step, sums, turn=turn, base=base, grads=grads, top=top):
+
+        def value_body(step, none, turn=turn, base=base, grads=grads):
+            kp = leaving(turn, step)
+            for s in range(rows // SUB):
+                here = slice(s * SUB, (s + 1) * SUB)
+                weight = s_buf[turn, kp, here, :] * inverses[turn]
+                s_buf[turn, kp, here, :] = weight
+                wl_buf[here, :] = weight.astype(BF16)
+            place = block(base + kp, rows)
+            dkv_acc[1, place, :] += jnp.dot(wl_buf[...], grads, preferred_element_type=F32)
+            if turn == 1:
+                send_pair(1, kp)
+            return none
+
+        lax.fori_loop(0, at_pair + 1, value_body, 0)
+
+    for turn, (half, at_pair, base) in enumerate(halves):
+        queries = q_buf[block(half, rows), :]
+        grads = g_buf[block(half, rows), :]
+
+        def prob_body(step, num, turn=turn, base=base, grads=grads):
             kp = arrival(turn, step)
             wait_new(turn, 1, kp)
-            den, num = sums
             for s in range(rows // SUB):
                 here = slice(s * SUB, (s + 1) * SUB)
                 vals = kv_buf[1, pl.ds(pl.multiple_of((base + kp) * rows + s * SUB, SUB), SUB), :]
                 prob = nt(vals, grads)
-                weight = jnp.exp2(s_buf[turn, kp, here, :] - top)
-                s_buf[turn, kp, here, :] = weight
                 p_buf[kp, here, :] = prob
-                den = den + jnp.sum(folded(weight), axis=0)
-                num = num + jnp.sum(folded(weight * prob), axis=0)
-            return den, num
-
-        zero = jnp.zeros((8, rows), F32)
-        den, num = lax.fori_loop(0, at_pair + 1, weigh_body, (zero, zero))
-        inverse = 1.0 / jnp.sum(den, axis=0, keepdims=True)
-        delta = jnp.sum(num, axis=0, keepdims=True) * inverse
-
-        def grad_body(
-            step, total, turn=turn, at_pair=at_pair, base=base, queries=queries, grads=grads,
-            inverse=inverse, delta=delta,
-        ):
-            kp = step
-            if turn == 1:
-                kp = (step + jnp.where(straddle, 1, 0)) % (at_pair + 1)
+                num = num + jnp.sum(folded(s_buf[turn, kp, here, :] * prob), axis=0)
+            return num
+
+        num = lax.fori_loop(0, at_pair + 1, prob_body, zero)
+        delta = jnp.sum(num, axis=0, keepdims=True)
+
+        def grad_body(step, total, turn=turn, base=base, queries=queries, delta=delta):
+            kp = leaving(turn, step)
             for s in range(rows // SUB):
                 here = slice(s * SUB, (s + 1) * SUB)
-                weight = s_buf[turn, kp, here, :] * inverse
-                wl_buf[here, :] = weight.astype(BF16)
-                ds_buf[here, :] = (weight * (p_buf[kp, here, :] - delta)).astype(BF16)
+                ds_buf[here, :] = (
+                    s_buf[turn, kp, here, :] * (p_buf[kp, here, :] - delta)
+                ).astype(BF16)
             place = block(base + kp, rows)
             score_grad = ds_buf[...]
             dkv_acc[0, place, :] += jnp.dot(score_grad, queries, preferred_element_type=F32)
-            dkv_acc[1, place, :] += jnp.dot(wl_buf[...], grads, preferred_element_type=F32)
-            total = total + tn(kv_buf[0, place, :], score_grad)
             if turn == 1:
-                send_pair(kp)
-            return total
+                send_pair(0, kp)
+            return total + tn(kv_buf[0, place, :], score_grad)
 
         total = lax.fori_loop(0, at_pair + 1, grad_body, jnp.zeros((dim, rows), F32))
         dq_low[block(half, rows), :] = (total * score_scale).T.astype(BF16)
@@ -326,9 +350,10 @@
     if wide:
         @pl.when(straddle)
         def _():
-            round_pair(pairs)
-            for b in range(2):
-                send_slot(group + b, (4 * quad + b + 2) % n, turns)
+            for kind in range(2):
+                round_pair(kind, pairs)
+                for b in range(2):
+                    send_slot(kind, group + b, (4 * quad + b + 2) % n, turns)
 
     for j, at, needed, slot in turn_list:
         @pl.when(needed)
@@ -432,7 +457,7 @@
         out_shape=(out, out, out),
         in_specs=[flat, pl.BlockSpec((2, kinds, tok // steps, width), lambda i: (0, 0, i, 0))],
         out_specs=(flat, flat, flat),
-        compiler_params=pltpu.CompilerParams(vmem_limit_bytes=16 * 1024 * 1024),
+        compiler_params=pltpu.CompilerParams(vmem_limit_bytes=60 * 1024 * 1024),
     )(dq_raw, parts)
 
 

time: 58.5 us -> 55.1 us (0.942)
  the two profiles are of different devices: /device:TPU:30 before, /device:TPU:8 now
where the time goes in v3:
time: 55.1 us; the launch traced here: 54.9 us
  Pallas kernels  54.3 us (99%)
  between operations  0.64 us (1%)
    pallas_call x1, Pallas kernels, local(): pl.pallas_call(functools.partial(kernel, n), out_shape=(out, jax.ShapeDty...  52.2 us
    pallas_call x1, Pallas kernels, local(): pl.pallas_call(functools.partial(add_kernel, n, group), grid=(steps,), ou...  2.1 us

profile of v3, /device:TPU:8, one launch (start us, length us, event | category | flops | bytes accessed | tf_op | source)
XLA Modules:
  0.0 54.9 jit_solution(4344054044404741848)
XLA Ops:
  0.6 52.2 %shard_map.85 = (bf16[256,512]{1,0:T(8,128)(2,1)}, bf16[2,2,256,512]{3,2,1,0:T(8,128)(2,1)}) custom-call(bf16[256,512]{1,0:T(8,128)(2,1)} %q_ref.1, bf16[256,512]{1,0:T(8,128)(2,1)} %k_ref.1, bf16[256,512]{1,0:T(8,128)(2,1)} %v_ref.1, bf16[256,1024]{1,0:T(8,128)(2,1)} %og_ref.1, bf16[512,4096]{1,0:T(8,128)(2,1)} %w_hbm.1, s32[4,3]{1,0:T(4,128)} %off_ref.1), custom_call_target="tpu_custom_call" | custom-call | flops 2751463424 | bytes 6291456 | tf_op jit(solution)/shard_map/pallas_call | solution.py:421
  52.8 2.1 %shard_map.86 = (bf16[256,512]{1,0:T(8,128)(2,1)}, bf16[256,512]{1,0:T(8,128)(2,1)}, bf16[256,512]{1,0:T(8,128)(2,1)}) custom-call(bf16[256,512]{1,0:T(8,128)(2,1)} %get-tuple-element.5.dq_ref, bf16[2,2,256,512]{3,2,1,0:T(8,128)(2,1)} %get-tuple-element.6.part_ref), custom_call_target="tpu_custom_call" | custom-call | tf_op jit(solution)/shard_map/pallas_call | solution.py:454

commit v4 on v3

--- a/solution.py
+++ b/solution.py
@@ -38,9 +38,9 @@
 
 def kernel(
     n, q_ref, k_ref, v_ref, og_ref, w_hbm, off_ref, dq_ref, part_buf,
-    w_buf, og_buf, grad_buf, q_buf, g_buf, kv_buf, s_buf, p_buf, ds_buf, wl_buf,
+    w_buf, og_buf, stage, grad_buf, q_buf, g_buf, kv_buf, s_buf, p_buf, ds_buf, wl_buf,
     dkv_acc, dkv_low, dq_low,
-    w_sem, og_sem, og_send, og_recv, fw_send, fw_recv, pair_send, pair_recv,
+    w_sem, og_sem, stage_sem, og_send, og_recv, fw_send, fw_recv, pair_send, pair_recv,
     kv_send, kv_recv, q_send, q_recv, g_send, g_recv,
     dq_send, dq_recv, part_send, part_recv,
 ):
@@ -86,12 +86,16 @@
     def arrived(dst, recv):
         pltpu.make_async_copy(dst, dst, recv).wait()
 
-    def cols(index):
-        return pl.ds(pl.multiple_of(index * dim, dim), dim)
-
     def block(index, size):
         return pl.ds(pl.multiple_of(index * size, size), size)
 
+    staged = []
+    for kind, ref in enumerate((k_ref, v_ref, q_ref)):
+        for h in range(4):
+            staged.append(pltpu.make_async_copy(
+                ref.at[:, pl.ds(h * dim, dim)], stage.at[kind, h], stage_sem.at[kind, h]
+            ))
+            staged[-1].start()
     w_copy = pltpu.make_async_copy(w_hbm, w_buf, w_sem)
     w_copy.start()
     og_copy = pltpu.make_async_copy(og_ref, og_buf.at[3], og_sem)
@@ -120,7 +124,8 @@
         ).start()
     tp_copy(og_ref, og_buf.at[0], pair_send, pair_recv, core_peer).start()
 
-    sources = (k_ref, v_ref)
+    for copy in staged:
+        copy.wait()
     turn_list = owner_turns(group, wide, own_slot)
 
     def send_kv(act, kind, entry):
@@ -134,20 +139,18 @@
 
     def start_kv(kind, at, h, slot, target):
         move(
-            sources[kind].at[:, pl.ds(h * dim, dim)], kv_buf.at[kind, block(slot, tok)],
+            stage.at[kind, h], kv_buf.at[kind, block(slot, tok)],
             kv_send.at[kind, at, h], kv_recv.at[kind, slot], target,
         )
 
     send_kv(start_kv, 0, turn_list[0])
     for h in range(4):
         move(
-            q_ref.at[:, pl.ds(h * dim, dim)], q_buf.at[block(head, tok)],
+            stage.at[2, h], q_buf.at[block(head, tok)],
             q_send.at[h], q_recv.at[head], 4 * quad + h,
         )
-    send_kv(start_kv, 1, turn_list[0])
-    for kind in range(2):
-        for entry in turn_list[1:]:
-            send_kv(start_kv, kind, entry)
+    for entry in turn_list[1:]:
+        send_kv(start_kv, 0, entry)
 
     dkv_acc[...] = jnp.zeros_like(dkv_acc)
 
@@ -171,12 +174,15 @@
         part = pl.ds(c * piece, piece)
         arrived(og_buf.at[2, :, part], fw_recv.at[c])
         total += nt(og_buf[2, :, part], w_part(far_peer, c))
-    grad_buf[...] = total.astype(BF16)
     for h in range(4):
+        grad_buf[h] = total[:, h * dim:(h + 1) * dim].astype(BF16)
         move(
-            grad_buf.at[:, pl.ds(h * dim, dim)], g_buf.at[block(head, tok)],
+            grad_buf.at[h], g_buf.at[block(head, tok)],
             g_send.at[h], g_recv.at[head], 4 * quad + h,
         )
+
+    for entry in turn_list:
+        send_kv(start_kv, 1, entry)
 
     def wait_pair(kind, pair):
         for b in range(2):
@@ -253,7 +259,7 @@
 
     def send_slot(kind, slot, owner, at):
         move(
-            dkv_low.at[kind, block(slot, tok)], part_buf.at[kind, at, :, cols(head)],
+            dkv_low.at[kind, block(slot, tok)], part_buf.at[kind, at, head],
             part_send.at[kind, slot], part_recv.at[kind, at, head], owner,
         )
 
@@ -344,7 +350,7 @@
         dq_low[block(half, rows), :] = (total * score_scale).T.astype(BF16)
         for b in range(2):
             move(
-                dq_low.at[block(2 * half + b, tok)], dq_ref.at[:, cols(head)],
+                dq_low.at[block(2 * half + b, tok)], dq_ref.at[head],
                 dq_send.at[2 * half + b], dq_recv.at[head], 4 * quad + 2 * half + b,
             )
     if wide:
@@ -360,9 +366,9 @@
         def _(at=at):
             for kind in range(2):
                 for h in range(4):
-                    arrived(part_buf.at[kind, at, :, pl.ds(h * dim, dim)], part_recv.at[kind, at, h])
+                    arrived(part_buf.at[kind, at, h], part_recv.at[kind, at, h])
     for h in range(4):
-        arrived(dq_ref.at[:, pl.ds(h * dim, dim)], dq_recv.at[h])
+        arrived(dq_ref.at[h], dq_recv.at[h])
 
     for c in range(CHUNKS):
         part = pl.ds(c * piece, piece)
@@ -370,12 +376,12 @@
         pltpu.make_async_copy(og_ref.at[:, part], og_ref.at[:, part], fw_send.at[c]).wait()
     pltpu.make_async_copy(og_ref, og_ref, pair_send).wait()
     for h in range(4):
-        sent(q_ref.at[:, pl.ds(h * dim, dim)], q_send.at[h], 4 * quad + h)
-        sent(grad_buf.at[:, pl.ds(h * dim, dim)], g_send.at[h], 4 * quad + h)
+        sent(stage.at[2, h], q_send.at[h], 4 * quad + h)
+        sent(grad_buf.at[h], g_send.at[h], 4 * quad + h)
         sent(dq_low.at[pl.ds(h * tok, tok)], dq_send.at[h], 4 * quad + h)
 
     def kv_sent(kind, at, h, slot, target):
-        sent(sources[kind].at[:, pl.ds(h * dim, dim)], kv_send.at[kind, at, h], target)
+        sent(stage.at[kind, h], kv_send.at[kind, at, h], target)
 
     for kind in range(2):
         for entry in turn_list:
@@ -393,13 +399,16 @@
 
 def add_kernel(n, group, dq_ref, part_ref, dq_out, dk_out, dv_out):
     own_slot = ((lax.axis_index("ctx") + n - 2) % n) % group
-    dq_out[...] = dq_ref[...]
-    for kind, out in ((0, dk_out), (1, dv_out)):
-        total = None
-        for j, at, needed, slot in owner_turns(group, n > group, own_slot):
-            part = part_ref[kind, at].astype(F32)
-            total = part if total is None else total + jnp.where(needed, part, 0.0)
-        out[...] = total.astype(BF16)
+    dim = dq_ref.shape[2]
+    for h in range(4):
+        here = slice(h * dim, (h + 1) * dim)
+        dq_out[:, here] = dq_ref[h]
+        for kind, out in ((0, dk_out), (1, dv_out)):
+            total = None
+            for j, at, needed, slot in owner_turns(group, n > group, own_slot):
+                part = part_ref[kind, at, h].astype(F32)
+                total = part if total is None else total + jnp.where(needed, part, 0.0)
+            out[:, here] = total.astype(BF16)
 
 
 def local(queries, keys, values, out_grad, w_out, offsets):
@@ -420,13 +429,17 @@
     hbm = pl.BlockSpec(memory_space=pl.ANY)
     dq_raw, parts = pl.pallas_call(
         functools.partial(kernel, n),
-        out_shape=(out, jax.ShapeDtypeStruct((2, kinds, tok, width), BF16)),
+        out_shape=(
+            jax.ShapeDtypeStruct((4, tok, dim), BF16),
+            jax.ShapeDtypeStruct((2, kinds, 4, tok, dim), BF16),
+        ),
         in_specs=[hbm] * 5 + [pl.BlockSpec(memory_space=pltpu.SMEM)],
         out_specs=(hbm, hbm),
         scratch_shapes=[
             pltpu.VMEM(w_out.shape, BF16),
             pltpu.VMEM((4, tok, feats), BF16),
-            pltpu.VMEM((tok, width), BF16),
+            pltpu.VMEM((3, 4, tok, dim), BF16),
+            pltpu.VMEM((4, tok, dim), BF16),
             pltpu.VMEM((4 * tok, dim), BF16),
             pltpu.VMEM((4 * tok, dim), BF16),
             pltpu.VMEM((2, slots * tok, dim), BF16),
@@ -437,7 +450,7 @@
             pltpu.VMEM((2, slots * tok, dim), F32),
             pltpu.VMEM((2, slots * tok, dim), BF16),
             pltpu.VMEM((4 * tok, dim), BF16),
-            dma, dma, dma((CHUNKS,)), dma((CHUNKS,)), dma((CHUNKS,)), dma((CHUNKS,)), dma, dma,
+            dma, dma, dma((3, 4)), dma((CHUNKS,)), dma((CHUNKS,)), dma((CHUNKS,)), dma((CHUNKS,)), dma, dma,
             dma((2, kinds, 4)), dma((2, slots)), dma((4,)), dma((4,)), dma((4,)), dma((4,)),
             dma((4,)), dma((4,)), dma((2, slots)), dma((2, kinds, 4)),
         ],
@@ -455,7 +468,10 @@
         functools.partial(add_kernel, n, group),
         grid=(steps,),
         out_shape=(out, out, out),
-        in_specs=[flat, pl.BlockSpec((2, kinds, tok // steps, width), lambda i: (0, 0, i, 0))],
+        in_specs=[
+            pl.BlockSpec((4, tok // steps, dim), lambda i: (0, i, 0)),
+            pl.BlockSpec((2, kinds, 4, tok // steps, dim), lambda i: (0, 0, 0, i, 0)),
+        ],
         out_specs=(flat, flat, flat),
         compiler_params=pltpu.CompilerParams(vmem_limit_bytes=60 * 1024 * 1024),
     )(dq_raw, parts)

time: 55.1 us -> 56.2 us (1.020)
  Pallas kernels: 54.3 us -> 55.4 us
    pallas_call x1, Pallas kernels: 52.2 us -> 53.3 us  [local(): pl.pallas_call(functools.partial(kernel, n), out_shape=(jax.ShapeDtypeStr...]
where the time goes in v4:
time: 56.2 us; the launch traced here: 56 us
  Pallas kernels  55.4 us (99%)
  between operations  0.64 us (1%)
    pallas_call x1, Pallas kernels, local(): pl.pallas_call(functools.partial(kernel, n), out_shape=(jax.ShapeDtypeStr...  53.3 us
    pallas_call x1, Pallas kernels, local(): pl.pallas_call(functools.partial(add_kernel, n, group), grid=(steps,), ou...  2.13 us

profile of v4, /device:TPU:8, one launch (start us, length us, event | category | flops | bytes accessed | tf_op | source)
XLA Modules:
  0.0 56.0 jit_solution(3979757773621998279)
XLA Ops:
  0.6 53.3 %shard_map.85 = (bf16[4,256,128]{2,1,0:T(8,128)(2,1)}, bf16[2,2,4,256,128]{4,3,2,1,0:T(8,128)(2,1)}) custom-call(bf16[256,512]{1,0:T(8,128)(2,1)} %q_ref.1, bf16[256,512]{1,0:T(8,128)(2,1)} %k_ref.1, bf16[256,512]{1,0:T(8,128)(2,1)} %v_ref.1, bf16[256,1024]{1,0:T(8,128)(2,1)} %og_ref.1, bf16[512,4096]{1,0:T(8,128)(2,1)} %w_hbm.1, s32[4,3]{1,0:T(4,128)} %off_ref.1), custom_call_target="tpu_custom_call" | custom-call | flops 2751463424 | bytes 6291456 | tf_op jit(solution)/shard_map/pallas_call | solution.py:430
  53.9 2.1 %shard_map.86 = (bf16[256,512]{1,0:T(8,128)(2,1)}, bf16[256,512]{1,0:T(8,128)(2,1)}, bf16[256,512]{1,0:T(8,128)(2,1)}) custom-call(bf16[4,256,128]{2,1,0:T(8,128)(2,1)} %get-tuple-element.5.dq_ref, bf16[2,2,4,256,128]{4,3,2,1,0:T(8,128)(2,1)} %get-tuple-element.6.part_ref), custom_call_target="tpu_custom_call" | custom-call | tf_op jit(solution)/shard_map/pallas_call | solution.py:467

commit v5 on v4

--- a/solution.py
+++ b/solution.py
@@ -13,7 +13,7 @@
 MESH = pl.DeviceIdType.MESH
 NEGATIVE_FILL = -1e30
 CHUNKS = 4
-SUB = 128
+SUB = 256
 F32 = jnp.float32
 BF16 = jnp.bfloat16
 
@@ -151,6 +151,7 @@
         )
     for entry in turn_list[1:]:
         send_kv(start_kv, 0, entry)
+    send_kv(start_kv, 1, turn_list[0])
 
     dkv_acc[...] = jnp.zeros_like(dkv_acc)
 
@@ -181,7 +182,7 @@
             g_send.at[h], g_recv.at[head], 4 * quad + h,
         )
 
-    for entry in turn_list:
+    for entry in turn_list[1:]:
         send_kv(start_kv, 1, entry)
 
     def wait_pair(kind, pair):
@@ -208,8 +209,7 @@
     halves = [(early, first_pair, first_base), (1 - early, last_pair, 0)]
 
     def arrival(turn, step):
-        count = halves[turn][1] + 1
-        return step if turn == 0 else (step + jnp.where(straddle, count - 1, 1)) % count
+        return step if turn == 0 else jnp.where(straddle, step, last_pair - 1 - step)
 
     def wait_new(turn, kind, kp):
         if turn == 0:
@@ -223,12 +223,11 @@
     def folded(values):
         return values.reshape(values.shape[0] // 8, 8, values.shape[1])
 
-    tops = []
+    logs = []
     for turn, (half, at_pair, base) in enumerate(halves):
         queries = q_buf[block(half, rows), :]
 
-        def score_body(step, top, turn=turn, at_pair=at_pair, base=base, queries=queries):
-            kp = arrival(turn, step)
+        def score_tile(kp, state, causal, turn=turn, at_pair=at_pair, base=base, queries=queries):
             wait_new(turn, 0, kp)
             same0 = jnp.where(at_pair // 2 == kp // 2, 1.0, 0.0)
             same1 = jnp.where(at_pair // 4 == kp // 4, 1.0, 0.0)
@@ -237,20 +236,31 @@
                 count > 2.5, math.log2(3.0),
                 jnp.where(count > 1.5, 1.0, jnp.where(count > 0.5, 0.0, NEGATIVE_FILL)),
             )
-            lead = (at_pair - kp) * rows
+            top, den = state
             for s in range(rows // SUB):
                 keys = kv_buf[0, pl.ds(pl.multiple_of((base + kp) * rows + s * SUB, SUB), SUB), :]
                 scores = folded(nt(keys, queries) * to_exp2) + bias[None]
-                scores = scores.reshape(SUB, rows)
-                scores = jnp.where(sub_row + s * SUB <= sub_col + lead, scores, NEGATIVE_FILL)
-                s_buf[turn, kp, s * SUB:(s + 1) * SUB, :] = scores
-                top = jnp.maximum(top, jnp.max(folded(scores), axis=0))
-            return top
-
-        top = lax.fori_loop(
-            0, at_pair + 1, score_body, jnp.full((8, rows), NEGATIVE_FILL, F32)
-        )
-        tops.append(jnp.max(top, axis=0, keepdims=True))
+                if causal:
+                    scores = scores.reshape(SUB, rows)
+                    scores = folded(jnp.where(sub_row + s * SUB <= sub_col, scores, NEGATIVE_FILL))
+                s_buf[turn, kp, s * SUB:(s + 1) * SUB, :] = scores.reshape(SUB, rows)
+                new_top = jnp.maximum(top, jnp.max(scores, axis=0))
+                den = den * jnp.exp2(top - new_top) + jnp.sum(
+                    jnp.exp2(scores - new_top[None]), axis=0
+                )
+                top = new_top
+            return top, den
+
+        state = (jnp.full((8, rows), NEGATIVE_FILL, F32), jnp.zeros((8, rows), F32))
+        state = score_tile(at_pair, state, True)
+        top, den = lax.fori_loop(
+            0, at_pair,
+            lambda step, state, turn=turn, tile=score_tile: tile(arrival(turn, step), state, False),
+            state,
+        )
+        row_top = jnp.max(top, axis=0, keepdims=True)
+        row_total = jnp.sum(den * jnp.exp2(top - row_top), axis=0, keepdims=True)
+        logs.append(row_top + jnp.log2(row_total))
 
     part_at = jnp.where(straddle, turns, start // 4) - 1
 
@@ -281,45 +291,23 @@
         return (step + jnp.where(straddle, 1, 0)) % (halves[1][1] + 1)
 
     zero = jnp.zeros((8, rows), F32)
-    inverses = []
-    for turn, (half, at_pair, base) in enumerate(halves):
-        def weigh_body(step, den, turn=turn, top=tops[turn]):
-            for s in range(rows // SUB):
-                here = slice(s * SUB, (s + 1) * SUB)
-                weight = jnp.exp2(s_buf[turn, step, here, :] - top)
-                s_buf[turn, step, here, :] = weight
-                den = den + jnp.sum(folded(weight), axis=0)
-            return den
-
-        den = lax.fori_loop(0, at_pair + 1, weigh_body, zero)
-        inverses.append(1.0 / jnp.sum(den, axis=0, keepdims=True))
-
     for turn, (half, at_pair, base) in enumerate(halves):
         for b in range(2):
             arrived(g_buf.at[block(2 * half + b, tok)], g_recv.at[2 * half + b])
+        queries = q_buf[block(half, rows), :]
         grads = g_buf[block(half, rows), :]
 
-        def value_body(step, none, turn=turn, base=base, grads=grads):
+        def weigh_body(step, num, turn=turn, base=base, grads=grads):
             kp = leaving(turn, step)
             for s in range(rows // SUB):
                 here = slice(s * SUB, (s + 1) * SUB)
-                weight = s_buf[turn, kp, here, :] * inverses[turn]
+                weight = jnp.exp2(s_buf[turn, kp, here, :] - logs[turn])
                 s_buf[turn, kp, here, :] = weight
                 wl_buf[here, :] = weight.astype(BF16)
             place = block(base + kp, rows)
             dkv_acc[1, place, :] += jnp.dot(wl_buf[...], grads, preferred_element_type=F32)
             if turn == 1:
                 send_pair(1, kp)
-            return none
-
-        lax.fori_loop(0, at_pair + 1, value_body, 0)
-
-    for turn, (half, at_pair, base) in enumerate(halves):
-        queries = q_buf[block(half, rows), :]
-        grads = g_buf[block(half, rows), :]
-
-        def prob_body(step, num, turn=turn, base=base, grads=grads):
-            kp = arrival(turn, step)
             wait_new(turn, 1, kp)
             for s in range(rows // SUB):
                 here = slice(s * SUB, (s + 1) * SUB)
@@ -329,7 +317,7 @@
                 num = num + jnp.sum(folded(s_buf[turn, kp, here, :] * prob), axis=0)
             return num
 
-        num = lax.fori_loop(0, at_pair + 1, prob_body, zero)
+        num = lax.fori_loop(0, at_pair + 1, weigh_body, zero)
         delta = jnp.sum(num, axis=0, keepdims=True)
 
         def grad_body(step, total, turn=turn, base=base, queries=queries, delta=delta):

time: 56.2 us -> 55.6 us (0.989)
  Pallas kernels: 55.4 us -> 54.8 us
    pallas_call x1, Pallas kernels: 53.3 us -> 52.6 us  [local(): pl.pallas_call(functools.partial(kernel, n), out_shape=(jax.ShapeDtypeStr...]
where the time goes in v5:
time: 55.6 us; the launch traced here: 55.4 us
  Pallas kernels  54.8 us (99%)
  between operations  0.64 us (1%)
    pallas_call x1, Pallas kernels, local(): pl.pallas_call(functools.partial(kernel, n), out_shape=(jax.ShapeDtypeStr...  52.6 us
    pallas_call x1, Pallas kernels, local(): pl.pallas_call(functools.partial(add_kernel, n, group), grid=(steps,), ou...  2.13 us

profile of v5, /device:TPU:8, one launch (start us, length us, event | category | flops | bytes accessed | tf_op | source)
XLA Modules:
  0.0 55.4 jit_solution(1909040500960325586)
XLA Ops:
  0.6 52.6 %shard_map.85 = (bf16[4,256,128]{2,1,0:T(8,128)(2,1)}, bf16[2,2,4,256,128]{4,3,2,1,0:T(8,128)(2,1)}) custom-call(bf16[256,512]{1,0:T(8,128)(2,1)} %q_ref.1, bf16[256,512]{1,0:T(8,128)(2,1)} %k_ref.1, bf16[256,512]{1,0:T(8,128)(2,1)} %v_ref.1, bf16[256,1024]{1,0:T(8,128)(2,1)} %og_ref.1, bf16[512,4096]{1,0:T(8,128)(2,1)} %w_hbm.1, s32[4,3]{1,0:T(4,128)} %off_ref.1), custom_call_target="tpu_custom_call" | custom-call | flops 2751463424 | bytes 6291456 | tf_op jit(solution)/shard_map/pallas_call | solution.py:418
  53.3 2.1 %shard_map.86 = (bf16[256,512]{1,0:T(8,128)(2,1)}, bf16[256,512]{1,0:T(8,128)(2,1)}, bf16[256,512]{1,0:T(8,128)(2,1)}) custom-call(bf16[4,256,128]{2,1,0:T(8,128)(2,1)} %get-tuple-element.5.dq_ref, bf16[2,2,4,256,128]{4,3,2,1,0:T(8,128)(2,1)} %get-tuple-element.6.part_ref), custom_call_target="tpu_custom_call" | custom-call | tf_op jit(solution)/shard_map/pallas_call | solution.py:455

commit v6 on v5

--- a/solution.py
+++ b/solution.py
@@ -38,7 +38,7 @@
 
 def kernel(
     n, q_ref, k_ref, v_ref, og_ref, w_hbm, off_ref, dq_ref, part_buf,
-    w_buf, og_buf, stage, grad_buf, q_buf, g_buf, kv_buf, s_buf, p_buf, ds_buf, wl_buf,
+    w_buf, og_buf, stage, grad_buf, q_buf, g_buf, kv_buf, s_buf, p_buf, ds_buf, wl_buf, turned_buf,
     dkv_acc, dkv_low, dq_low,
     w_sem, og_sem, stage_sem, og_send, og_recv, fw_send, fw_recv, pair_send, pair_recv,
     kv_send, kv_recv, q_send, q_recv, g_send, g_recv,
@@ -161,22 +161,22 @@
     def w_part(shard, c):
         return w_buf[:, pl.ds(pl.multiple_of(shard * feats + c * piece, piece), piece)]
 
-    total = nt(og_buf[3], w_buf[:, block(tp, feats)])
+    total = nt(w_buf[:, block(tp, feats)], og_buf[3])
     arrived(og_buf.at[0], pair_recv)
-    total += nt(og_buf[0], w_buf[:, block(core_peer, feats)])
+    total += nt(w_buf[:, block(core_peer, feats)], og_buf[0])
     for c in range(CHUNKS):
         part = pl.ds(c * piece, piece)
         arrived(og_buf.at[1, :, part], og_recv.at[c])
         tp_copy(
             og_buf.at[1, :, part], og_buf.at[2, :, part], fw_send.at[c], fw_recv.at[c], core_peer
         ).start()
-        total += nt(og_buf[1, :, part], w_part(y_peer, c))
+        total += nt(w_part(y_peer, c), og_buf[1, :, part])
     for c in range(CHUNKS):
         part = pl.ds(c * piece, piece)
         arrived(og_buf.at[2, :, part], fw_recv.at[c])
-        total += nt(og_buf[2, :, part], w_part(far_peer, c))
+        total += nt(w_part(far_peer, c), og_buf[2, :, part])
     for h in range(4):
-        grad_buf[h] = total[:, h * dim:(h + 1) * dim].astype(BF16)
+        grad_buf[h] = total[h * dim:(h + 1) * dim, :].T.astype(BF16)
         move(
             grad_buf.at[h], g_buf.at[block(head, tok)],
             g_send.at[h], g_recv.at[head], 4 * quad + h,
@@ -227,6 +227,8 @@
     for turn, (half, at_pair, base) in enumerate(halves):
         queries = q_buf[block(half, rows), :]
 
+        turned_buf[...] = queries.T
+
         def score_tile(kp, state, causal, turn=turn, at_pair=at_pair, base=base, queries=queries):
             wait_new(turn, 0, kp)
             same0 = jnp.where(at_pair // 2 == kp // 2, 1.0, 0.0)
@@ -239,7 +241,7 @@
             top, den = state
             for s in range(rows // SUB):
                 keys = kv_buf[0, pl.ds(pl.multiple_of((base + kp) * rows + s * SUB, SUB), SUB), :]
-                scores = folded(nt(keys, queries) * to_exp2) + bias[None]
+                scores = folded(jnp.dot(keys, turned_buf[...], preferred_element_type=F32) * to_exp2) + bias[None]
                 if causal:
                     scores = scores.reshape(SUB, rows)
                     scores = folded(jnp.where(sub_row + s * SUB <= sub_col, scores, NEGATIVE_FILL))
@@ -296,6 +298,8 @@
             arrived(g_buf.at[block(2 * half + b, tok)], g_recv.at[2 * half + b])
         queries = q_buf[block(half, rows), :]
         grads = g_buf[block(half, rows), :]
+
+        turned_buf[...] = grads.T
 
         def weigh_body(step, num, turn=turn, base=base, grads=grads):
             kp = leaving(turn, step)
@@ -312,7 +316,7 @@
             for s in range(rows // SUB):
                 here = slice(s * SUB, (s + 1) * SUB)
                 vals = kv_buf[1, pl.ds(pl.multiple_of((base + kp) * rows + s * SUB, SUB), SUB), :]
-                prob = nt(vals, grads)
+                prob = jnp.dot(vals, turned_buf[...], preferred_element_type=F32)
                 p_buf[kp, here, :] = prob
                 num = num + jnp.sum(folded(s_buf[turn, kp, here, :] * prob), axis=0)
             return num
@@ -435,6 +439,7 @@
             pltpu.VMEM((pairs, rows, rows), F32),
             pltpu.VMEM((rows, rows), BF16),
             pltpu.VMEM((rows, rows), BF16),
+            pltpu.VMEM((dim, rows), BF16),
             pltpu.VMEM((2, slots * tok, dim), F32),
             pltpu.VMEM((2, slots * tok, dim), BF16),
             pltpu.VMEM((4 * tok, dim), BF16),

time: 55.6 us -> 55.6 us (level)
  no operation moved by 1% of the time
where the time goes in v6:
time: 55.6 us; the launch traced here: 55.4 us
  Pallas kernels  54.8 us (99%)
  between operations  0.64 us (1%)
    pallas_call x1, Pallas kernels, local(): pl.pallas_call(functools.partial(kernel, n), out_shape=(jax.ShapeDtypeStr...  52.6 us
    pallas_call x1, Pallas kernels, local(): pl.pallas_call(functools.partial(add_kernel, n, group), grid=(steps,), ou...  2.13 us

profile of v6, /device:TPU:8, one launch (start us, length us, event | category | flops | bytes accessed | tf_op | source)
XLA Modules:
  0.0 55.4 jit_solution(11020199245971943686)
XLA Ops:
  0.6 52.6 %shard_map.85 = (bf16[4,256,128]{2,1,0:T(8,128)(2,1)}, bf16[2,2,4,256,128]{4,3,2,1,0:T(8,128)(2,1)}) custom-call(bf16[256,512]{1,0:T(8,128)(2,1)} %q_ref.1, bf16[256,512]{1,0:T(8,128)(2,1)} %k_ref.1, bf16[256,512]{1,0:T(8,128)(2,1)} %v_ref.1, bf16[256,1024]{1,0:T(8,128)(2,1)} %og_ref.1, bf16[512,4096]{1,0:T(8,128)(2,1)} %w_hbm.1, s32[4,3]{1,0:T(4,128)} %off_ref.1), custom_call_target="tpu_custom_call" | custom-call | flops 2751463424 | bytes 6291456 | tf_op jit(solution)/shard_map/pallas_call | solution.py:422
  53.3 2.1 %shard_map.86 = (bf16[256,512]{1,0:T(8,128)(2,1)}, bf16[256,512]{1,0:T(8,128)(2,1)}, bf16[256,512]{1,0:T(8,128)(2,1)}) custom-call(bf16[4,256,128]{2,1,0:T(8,128)(2,1)} %get-tuple-element.5.dq_ref, bf16[2,2,4,256,128]{4,3,2,1,0:T(8,128)(2,1)} %get-tuple-element.6.part_ref), custom_call_target="tpu_custom_call" | custom-call | tf_op jit(solution)/shard_map/pallas_call | solution.py:460

commit v7 on v6

--- a/solution.py
+++ b/solution.py
@@ -227,7 +227,7 @@
     for turn, (half, at_pair, base) in enumerate(halves):
         queries = q_buf[block(half, rows), :]
 
-        turned_buf[...] = queries.T
+        turned_buf[turn] = queries.T
 
         def score_tile(kp, state, causal, turn=turn, at_pair=at_pair, base=base, queries=queries):
             wait_new(turn, 0, kp)
@@ -241,7 +241,7 @@
             top, den = state
             for s in range(rows // SUB):
                 keys = kv_buf[0, pl.ds(pl.multiple_of((base + kp) * rows + s * SUB, SUB), SUB), :]
-                scores = folded(jnp.dot(keys, turned_buf[...], preferred_element_type=F32) * to_exp2) + bias[None]
+                scores = folded(jnp.dot(keys, turned_buf[turn], preferred_element_type=F32) * to_exp2) + bias[None]
                 if causal:
                     scores = scores.reshape(SUB, rows)
                     scores = folded(jnp.where(sub_row + s * SUB <= sub_col, scores, NEGATIVE_FILL))
@@ -293,13 +293,14 @@
         return (step + jnp.where(straddle, 1, 0)) % (halves[1][1] + 1)
 
     zero = jnp.zeros((8, rows), F32)
+    bodies = []
     for turn, (half, at_pair, base) in enumerate(halves):
         for b in range(2):
             arrived(g_buf.at[block(2 * half + b, tok)], g_recv.at[2 * half + b])
         queries = q_buf[block(half, rows), :]
         grads = g_buf[block(half, rows), :]
 
-        turned_buf[...] = grads.T
+        turned_buf[turn] = grads.T
 
         def weigh_body(step, num, turn=turn, base=base, grads=grads):
             kp = leaving(turn, step)
@@ -316,20 +317,29 @@
             for s in range(rows // SUB):
                 here = slice(s * SUB, (s + 1) * SUB)
                 vals = kv_buf[1, pl.ds(pl.multiple_of((base + kp) * rows + s * SUB, SUB), SUB), :]
-                prob = jnp.dot(vals, turned_buf[...], preferred_element_type=F32)
-                p_buf[kp, here, :] = prob
+                prob = jnp.dot(vals, turned_buf[turn], preferred_element_type=F32)
+                p_buf[turn, kp, here, :] = prob
                 num = num + jnp.sum(folded(s_buf[turn, kp, here, :] * prob), axis=0)
             return num
 
-        num = lax.fori_loop(0, at_pair + 1, weigh_body, zero)
-        delta = jnp.sum(num, axis=0, keepdims=True)
+        bodies.append(weigh_body)
+
+    ahead = jnp.where(straddle, pairs - 2, 0)
+    num_last = lax.fori_loop(0, ahead, bodies[1], zero)
+    num_first = lax.fori_loop(0, first_pair + 1, bodies[0], zero)
+    num_last = lax.fori_loop(ahead, last_pair + 1, bodies[1], num_last)
+    nums = (num_first, num_last)
+
+    for turn, (half, at_pair, base) in enumerate(halves):
+        queries = q_buf[block(half, rows), :]
+        delta = jnp.sum(nums[turn], axis=0, keepdims=True)
 
         def grad_body(step, total, turn=turn, base=base, queries=queries, delta=delta):
             kp = leaving(turn, step)
             for s in range(rows // SUB):
                 here = slice(s * SUB, (s + 1) * SUB)
                 ds_buf[here, :] = (
-                    s_buf[turn, kp, here, :] * (p_buf[kp, here, :] - delta)
+                    s_buf[turn, kp, here, :] * (p_buf[turn, kp, here, :] - delta)
                 ).astype(BF16)
             place = block(base + kp, rows)
             score_grad = ds_buf[...]
@@ -436,10 +446,10 @@
             pltpu.VMEM((4 * tok, dim), BF16),
             pltpu.VMEM((2, slots * tok, dim), BF16),
             pltpu.VMEM((2, pairs, rows, rows), F32),
-            pltpu.VMEM((pairs, rows, rows), F32),
+            pltpu.VMEM((2, pairs, rows, rows), F32),
             pltpu.VMEM((rows, rows), BF16),
             pltpu.VMEM((rows, rows), BF16),
-            pltpu.VMEM((dim, rows), BF16),
+            pltpu.VMEM((2, dim, rows), BF16),
             pltpu.VMEM((2, slots * tok, dim), F32),
             pltpu.VMEM((2, slots * tok, dim), BF16),
             pltpu.VMEM((4 * tok, dim), BF16),

time: 55.6 us -> 54.8 us (0.986)
  Pallas kernels: 54.8 us -> 54 us
    pallas_call x1, Pallas kernels: 52.6 us -> 51.8 us  [local(): pl.pallas_call(functools.partial(kernel, n), out_shape=(jax.ShapeDtypeStr...]
where the time goes in v7:
time: 54.8 us; the launch traced here: 54.6 us
  Pallas kernels  54 us (99%)
  between operations  0.64 us (1%)
    pallas_call x1, Pallas kernels, local(): pl.pallas_call(functools.partial(kernel, n), out_shape=(jax.ShapeDtypeStr...  51.8 us
    pallas_call x1, Pallas kernels, local(): pl.pallas_call(functools.partial(add_kernel, n, group), grid=(steps,), ou...  2.13 us

profile of v7, /device:TPU:8, one launch (start us, length us, event | category | flops | bytes accessed | tf_op | source)
XLA Modules:
  0.0 54.6 jit_solution(10888787138010560276)
XLA Ops:
  0.6 51.8 %shard_map.85 = (bf16[4,256,128]{2,1,0:T(8,128)(2,1)}, bf16[2,2,4,256,128]{4,3,2,1,0:T(8,128)(2,1)}) custom-call(bf16[256,512]{1,0:T(8,128)(2,1)} %q_ref.1, bf16[256,512]{1,0:T(8,128)(2,1)} %k_ref.1, bf16[256,512]{1,0:T(8,128)(2,1)} %v_ref.1, bf16[256,1024]{1,0:T(8,128)(2,1)} %og_ref.1, bf16[512,4096]{1,0:T(8,128)(2,1)} %w_hbm.1, s32[4,3]{1,0:T(4,128)} %off_ref.1), custom_call_target="tpu_custom_call" | custom-call | flops 2751463424 | bytes 6291456 | tf_op jit(solution)/shard_map/pallas_call | solution.py:432
  52.5 2.1 %shard_map.86 = (bf16[256,512]{1,0:T(8,128)(2,1)}, bf16[256,512]{1,0:T(8,128)(2,1)}, bf16[256,512]{1,0:T(8,128)(2,1)}) custom-call(bf16[4,256,128]{2,1,0:T(8,128)(2,1)} %get-tuple-element.5.dq_ref, bf16[2,2,4,256,128]{4,3,2,1,0:T(8,128)(2,1)} %get-tuple-element.6.part_ref), custom_call_target="tpu_custom_call" | custom-call | tf_op jit(solution)/shard_map/pallas_call | solution.py:470

commit v8 on v7

--- a/solution.py
+++ b/solution.py
@@ -164,27 +164,6 @@
     total = nt(w_buf[:, block(tp, feats)], og_buf[3])
     arrived(og_buf.at[0], pair_recv)
     total += nt(w_buf[:, block(core_peer, feats)], og_buf[0])
-    for c in range(CHUNKS):
-        part = pl.ds(c * piece, piece)
-        arrived(og_buf.at[1, :, part], og_recv.at[c])
-        tp_copy(
-            og_buf.at[1, :, part], og_buf.at[2, :, part], fw_send.at[c], fw_recv.at[c], core_peer
-        ).start()
-        total += nt(w_part(y_peer, c), og_buf[1, :, part])
-    for c in range(CHUNKS):
-        part = pl.ds(c * piece, piece)
-        arrived(og_buf.at[2, :, part], fw_recv.at[c])
-        total += nt(w_part(far_peer, c), og_buf[2, :, part])
-    for h in range(4):
-        grad_buf[h] = total[h * dim:(h + 1) * dim, :].T.astype(BF16)
-        move(
-            grad_buf.at[h], g_buf.at[block(head, tok)],
-            g_send.at[h], g_recv.at[head], 4 * quad + h,
-        )
-
-    for entry in turn_list[1:]:
-        send_kv(start_kv, 1, entry)
-
     def wait_pair(kind, pair):
         for b in range(2):
             slot = 2 * pair + b
@@ -263,6 +242,27 @@
         row_top = jnp.max(top, axis=0, keepdims=True)
         row_total = jnp.sum(den * jnp.exp2(top - row_top), axis=0, keepdims=True)
         logs.append(row_top + jnp.log2(row_total))
+
+    for c in range(CHUNKS):
+        part = pl.ds(c * piece, piece)
+        arrived(og_buf.at[1, :, part], og_recv.at[c])
+        tp_copy(
+            og_buf.at[1, :, part], og_buf.at[2, :, part], fw_send.at[c], fw_recv.at[c], core_peer
+        ).start()
+        total += nt(w_part(y_peer, c), og_buf[1, :, part])
+    for c in range(CHUNKS):
+        part = pl.ds(c * piece, piece)
+        arrived(og_buf.at[2, :, part], fw_recv.at[c])
+        total += nt(w_part(far_peer, c), og_buf[2, :, part])
+    for h in range(4):
+        grad_buf[h] = total[h * dim:(h + 1) * dim, :].T.astype(BF16)
+        move(
+            grad_buf.at[h], g_buf.at[block(head, tok)],
+            g_send.at[h], g_recv.at[head], 4 * quad + h,
+        )
+
+    for entry in turn_list[1:]:
+        send_kv(start_kv, 1, entry)
 
     part_at = jnp.where(straddle, turns, start // 4) - 1
 

time: 54.8 us -> 57.1 us (1.042)
  the two profiles are of different devices: /device:TPU:8 before, /device:TPU:27 now
where the time goes in v8:
time: 57.1 us; the launch traced here: 56.9 us
  Pallas kernels  56.3 us (99%)
  between operations  0.64 us (1%)
    pallas_call x1, Pallas kernels, local(): pl.pallas_call(functools.partial(kernel, n), out_shape=(jax.ShapeDtypeStr...  54.1 us
    pallas_call x1, Pallas kernels, local(): pl.pallas_call(functools.partial(add_kernel, n, group), grid=(steps,), ou...  2.13 us

profile of v8, /device:TPU:27, one launch (start us, length us, event | category | flops | bytes accessed | tf_op | source)
XLA Modules:
  0.0 56.9 jit_solution(6112578857874446064)
XLA Ops:
  0.6 54.1 %shard_map.85 = (bf16[4,256,128]{2,1,0:T(8,128)(2,1)}, bf16[2,2,4,256,128]{4,3,2,1,0:T(8,128)(2,1)}) custom-call(bf16[256,512]{1,0:T(8,128)(2,1)} %q_ref.1, bf16[256,512]{1,0:T(8,128)(2,1)} %k_ref.1, bf16[256,512]{1,0:T(8,128)(2,1)} %v_ref.1, bf16[256,1024]{1,0:T(8,128)(2,1)} %og_ref.1, bf16[512,4096]{1,0:T(8,128)(2,1)} %w_hbm.1, s32[4,3]{1,0:T(4,128)} %off_ref.1), custom_call_target="tpu_custom_call" | custom-call | flops 2751463424 | bytes 6291456 | tf_op jit(solution)/shard_map/pallas_call | solution.py:432
  54.8 2.1 %shard_map.86 = (bf16[256,512]{1,0:T(8,128)(2,1)}, bf16[256,512]{1,0:T(8,128)(2,1)}, bf16[256,512]{1,0:T(8,128)(2,1)}) custom-call(bf16[4,256,128]{2,1,0:T(8,128)(2,1)} %get-tuple-element.5.dq_ref, bf16[2,2,4,256,128]{4,3,2,1,0:T(8,128)(2,1)} %get-tuple-element.6.part_ref), custom_call_target="tpu_custom_call" | custom-call | tf_op jit(solution)/shard_map/pallas_call | solution.py:470
